TPU v7x, 32 devices: a whole 2x2x4 slice. The times are simulated.
32 devices in a mesh: dp: 8 (over z, x), tensor: 4 (over y, core).
Axes of the slice: x: 2, y: 2, z: 4, core: 2. Of those that a mesh axis runs over, the one named last changes fastest.
Arguments:
- enc_x: bfloat16 [4096, 1472], P(('dp', 'tensor')), may hold values from -6 to 6
- dec_x: bfloat16 [768, 1472], P(('dp', 'tensor')), may hold values from -6 to 6
- dec_cot: bfloat16 [768, 1472], P(('dp', 'tensor')), may hold values from -6 to 6
- item_count: int32 [8], P('dp'), may hold values from 1 to 4, as said below
- enc_mask: int32 [4096], P('dp'), may hold values from 0 to 1, as said below
- dec_mask: int32 [768], P('dp'), may hold values from 0 to 1, as said below
- enc_buckets: int32 [1023], replicated, may hold values from 0 to 31
- dec_buckets: int32 [96], replicated, may hold values from 0 to 31
- gains: float32 [6, 1472], replicated, may hold values from 0.25 to 1.75
- tables: float32 [2, 32, 6], replicated, may hold values from -4 to 4
- attn_qk: bfloat16 [3, 1472, 768], replicated, may hold values from -0.0625 to 0.0625
- attn_vo: bfloat16 [3, 1472, 768], replicated, may hold values from -0.5 to 0.5
- ff_in: bfloat16 [2, 2, 1472, 3584], P(None, None, None, 'tensor'), may hold values from -0.15625 to 0.15625
- ff_out: bfloat16 [2, 3584, 1472], P(None, 'tensor'), may hold values from -0.09375 to 0.09375
Outputs:
- dec_out: bfloat16 [768, 1472], P(('dp', 'tensor'))
- enc_grad: float32 [4096, 1472], P(('dp', 'tensor'))
- dec_grad: float32 [768, 1472], P(('dp', 'tensor'))
- gains_grad: float32 [6, 1472], replicated
- tables_grad: float32 [2, 32, 6], replicated
- qk_grad: float32 [3, 1472, 768], P(None, 'dp')
- vo_grad: float32 [3, 1472, 768], P(None, 'dp')
- ffin_grad: float32 [2, 2, 1472, 3584], P(None, None, 'dp', 'tensor')
- ffout_grad: float32 [2, 3584, 1472], P(None, 'tensor', 'dp')
Inputs may be any that keep to these rules, and one draw needn't show every extreme that they name: `item_count`: each entry is 1, 2 or 4, the number of equal items that a group's encoder rows and its target rows are cut into; every draw has a group with 1 item and one with 4. `enc_mask`: in each item the ones are a prefix holding at least half of the item (rounded down), never none. `dec_mask`: in each item the ones are a prefix holding at least half of the item (rounded down), never none. `enc_buckets`: entry k is the bucket of key place minus query place equal to k - 511. `dec_buckets`: entry k is the bucket of a key k places before its query.
All inputs are finite; a program needn't handle non-finite values.
Results may differ from a plain program's by a relative error of at most 0.03.
Values may be sent and summed in bfloat16 or wider, within the bound.
A program may use at most 256 MiB of HBM per device.

v0:
```python
import jax
import jax.numpy as jnp
from jax import lax
from jax.sharding import PartitionSpec as P

HEADS = 6
HEAD = 64
BUCKETS = 32


EPSILON = 1e-06
MASKED = -1000000000.0
HIGH = lax.Precision.HIGHEST


def norm_gain(rows, gain):
    return rows * lax.rsqrt(jnp.mean(rows * rows, axis=-1, keepdims=True) + EPSILON) * gain


def norm_back(rows, gain, grad_rows):
    unused, pullback = jax.vjp(norm_gain, rows, gain)
    return pullback(grad_rows)


def ff_act(gate, up_proj):
    return jax.nn.gelu(gate, approximate=True) * up_proj


def to_low(value):
    return value.astype(jnp.bfloat16)


def product(left, right):
    return jnp.dot(left, right, preferred_element_type=jnp.float32)


def product_over_rows(left, right):
    return lax.dot_general(
        left, right, (((0,), (0,)), ((), ())), preferred_element_type=jnp.float32
    )


def product_over_cols(left, right):
    return lax.dot_general(
        left, right, (((1,), (1,)), ((), ())), preferred_element_type=jnp.float32
    )


def gather_rows(rows):
    return lax.all_gather(rows, "tensor", axis=0, tiled=True)


def reduce_rows(rows):
    return lax.psum_scatter(rows, "tensor", scatter_dimension=0, tiled=True)


def gather_grads(rows):
    return lax.all_gather(rows, "tensor", axis=0, tiled=True)


def reduce_grads(rows):
    return lax.psum_scatter(rows, "tensor", scatter_dimension=0, tiled=True)


def tables_for(tensor_id):
    first = jnp.where(tensor_id < 2, 2 * tensor_id, tensor_id + 2)
    second = jnp.where(tensor_id < 2, 2 * tensor_id + 1, tensor_id + 2)
    keeping = jnp.where(tensor_id < 2, 1.0, 0.0).astype(jnp.float32)
    slot_rows = jnp.arange(2 * HEAD)
    head_of = jnp.where(slot_rows < HEAD, first, second)
    target = head_of * HEAD + slot_rows % HEAD
    factor = jnp.where(slot_rows < HEAD, 1.0, keeping)
    columns = jnp.arange(HEADS * HEAD)
    select = jnp.where(columns[None, :] == target[:, None], factor[:, None], 0.0)
    heads_all = jnp.arange(HEADS)
    slot_heads = jnp.stack([first, second])
    slot_keep = jnp.stack([jnp.ones((), jnp.float32), keeping])
    head_pick = jnp.where(heads_all[:, None] == slot_heads[None, :], slot_keep[None, :], 0.0)
    return (select, head_pick)


def attn_reduce(qk_slots, vo_slots, select_stack):
    qk_part, vo_part = (
        lax.psum_scatter(qk_slots, "dp", scatter_dimension=1, tiled=True),
        lax.psum_scatter(vo_slots, "dp", scatter_dimension=1, tiled=True),
    )
    qk_every, vo_every = (
        lax.all_gather(qk_part, "tensor", axis=2, tiled=True),
        lax.all_gather(vo_part, "tensor", axis=2, tiled=True),
    )

    def place(gathered):
        blocks, rows_here = (gathered.shape[0], gathered.shape[1])
        split = gathered.reshape(blocks, rows_here, select_stack.shape[0], 2, 2 * HEAD)
        placed = jnp.einsum("nrtac,tcj->nraj", split, select_stack, precision=HIGH)
        return placed.reshape(blocks, rows_here, 2 * select_stack.shape[2])

    return (place(qk_every), place(vo_every))


def offset_bias(buckets, slot_table):
    onehot = (buckets[:, None] == jnp.arange(BUCKETS)[None, :]).astype(jnp.float32)
    return (jnp.dot(onehot, slot_table, precision=HIGH).T, onehot)


def toeplitz(offset_terms, start, block, columns):
    period = 2 * columns
    wrapped = jnp.concatenate(
        [
            offset_terms[:, columns - 1 :],
            jnp.zeros((2, 1), jnp.float32),
            offset_terms[:, : columns - 1],
        ],
        axis=1,
    )
    doubled = jnp.concatenate([wrapped, wrapped], axis=1)
    shift = (period - start % period) % period
    rolled = lax.dynamic_slice_in_dim(doubled, shift, period, 1)
    tiled = jnp.tile(rolled, (1, block))[:, : block * (period - 1)]
    return tiled.reshape(2, block, period - 1)[:, :, :columns]


def enc_spread(offset_terms, start, block, columns):
    return toeplitz(offset_terms, start, block, columns)


def dec_spread(offset_terms, start, block, columns):
    whole = jnp.concatenate(
        [offset_terms[:, ::-1], jnp.broadcast_to(offset_terms[:, :1], (2, columns - 1))], axis=1
    )
    return toeplitz(whole, start, block, columns)


def make_extra(query_item, key_item, key_live, causal):

    def extra(start, block):
        row_place = start + jnp.arange(block)
        allowed = (query_item[:, None] == key_item[None, :]) & key_live[None, :]
        col_place = jnp.arange(key_item.shape[0])
        if causal:
            allowed = allowed & (col_place[None, :] <= row_place[:, None])
        return allowed

    return extra


def block_scores(query_block, key_heads, start, extra, spread, offset_terms):
    raw = jnp.einsum("rhd,shd->hrs", query_block, key_heads, preferred_element_type=jnp.float32)
    allowed = extra(start, query_block.shape[0])
    if spread is not None:
        raw = raw + spread(offset_terms, start, query_block.shape[0], key_heads.shape[0])
    return jnp.where(allowed[None], raw, MASKED)


def block_size(rows):
    return 512 if rows % 512 == 0 else rows


def attend(queries, keys, values, extra, spread, offset_terms):
    rows = queries.shape[0]
    block = block_size(rows)
    query_heads = queries.reshape(rows, 2, HEAD)
    key_heads = keys.reshape(keys.shape[0], 2, HEAD)
    value_heads = values.reshape(values.shape[0], 2, HEAD)

    def one_block(start):
        scores = block_scores(query_heads, key_heads, start, extra, spread, offset_terms)
        largest = jnp.max(scores, axis=-1, keepdims=True)
        shifted = jnp.exp(scores - largest)
        totals = jnp.sum(shifted, axis=-1, keepdims=True)
        weights = to_low(shifted / totals)
        mixed = jnp.einsum("hrs,shd->rhd", weights, value_heads, preferred_element_type=jnp.float32)
        return (mixed, (largest + jnp.log(totals))[..., 0])

    mixed, log_totals = lax.map(one_block, jnp.arange(rows // block) * block)
    return (mixed.reshape(rows, 2 * HEAD), log_totals)


def attend_back(queries, keys, values, log_totals, grad_out, extra, spread, offset_terms):
    rows = queries.shape[0]
    block = block_size(rows)
    key_count = keys.shape[0]
    query_heads = queries.reshape(rows, 2, HEAD)
    key_heads = keys.reshape(key_count, 2, HEAD)
    value_heads = values.reshape(values.shape[0], 2, HEAD)
    grad_heads = grad_out.reshape(rows, 2, HEAD)
    starts = jnp.arange(rows // block) * block
    if spread is None:
        offset_start = jnp.zeros((2, 1), jnp.float32)
    else:
        offset_start = jnp.zeros(offset_terms.shape, jnp.float32)

    def one_block(carry, inputs):
        grad_keys, grad_values, grad_offsets = carry
        start, log_total = inputs
        scores = block_scores(query_heads, key_heads, start, extra, spread, offset_terms)
        weights = jnp.exp(scores - log_total[..., None])
        grad_weights = jnp.einsum(
            "rhd,shd->hrs", grad_heads, value_heads, preferred_element_type=jnp.float32
        )
        weighted = jnp.sum(weights * grad_weights, axis=-1, keepdims=True)
        grad_scores = to_low(weights * (grad_weights - weighted))
        grad_query = jnp.einsum(
            "hrs,shd->rhd", grad_scores, key_heads, preferred_element_type=jnp.float32
        )
        grad_keys = grad_keys + jnp.einsum(
            "hrs,rhd->shd", grad_scores, query_heads, preferred_element_type=jnp.float32
        )
        grad_values = grad_values + jnp.einsum(
            "hrs,rhd->shd", to_low(weights), grad_heads, preferred_element_type=jnp.float32
        )
        if spread is not None:

            def bias_here(terms):
                return spread(terms, start, block, key_count)

            unused, pullback = jax.vjp(bias_here, offset_terms)
            grad_offsets = grad_offsets + pullback(grad_scores.astype(jnp.float32))[0]
        return ((grad_keys, grad_values, grad_offsets), grad_query)

    start_carry = (
        jnp.zeros(key_heads.shape, jnp.float32),
        jnp.zeros(value_heads.shape, jnp.float32),
        offset_start,
    )
    carried, grad_query = lax.scan(one_block, start_carry, (starts, log_totals))
    grad_keys, grad_values, grad_offsets = carried
    return (
        grad_query.reshape(rows, 2 * HEAD),
        grad_keys.reshape(key_count, 2 * HEAD),
        grad_values.reshape(values.shape[0], 2 * HEAD),
        grad_offsets,
    )


def attn_core(queries, keys, values, weight_out, extra, spread, offset_terms):
    mixed, log_totals = attend(queries, keys, values, extra, spread, offset_terms)
    mixed_low = to_low(mixed)
    return (
        product_over_cols(mixed_low, weight_out),
        (queries, keys, values, log_totals, mixed_low),
    )


def attn_core_back(grad_full, saved, weight_out, extra, spread, offset_terms):
    queries, keys, values, log_totals, mixed_low = saved
    grad_weight_out = product_over_rows(grad_full, mixed_low)
    grad_out = to_low(product(grad_full, weight_out))
    grad_query, grad_keys, grad_values, grad_offsets = attend_back(
        queries, keys, values, log_totals, grad_out, extra, spread, offset_terms
    )
    return (
        to_low(grad_query),
        to_low(grad_keys),
        to_low(grad_values),
        grad_weight_out,
        grad_offsets,
    )


def ff_forward(rows_full, weight_in, weight_out):
    gate = product(rows_full, weight_in[0])
    up_proj = product(rows_full, weight_in[1])
    hidden = to_low(ff_act(gate, up_proj))
    return (product(hidden, weight_out), (gate, up_proj, hidden))


def ff_back(grad_full, rows_full, saved, weight_in, weight_out):
    gate, up_proj, hidden = saved
    grad_weight_out = product_over_rows(hidden, grad_full)
    grad_hidden = product_over_cols(grad_full, weight_out)
    unused, pullback = jax.vjp(ff_act, gate, up_proj)
    grad_gate, grad_up = pullback(grad_hidden)
    grad_gate = to_low(grad_gate)
    grad_up = to_low(grad_up)
    grad_weight_in = jnp.stack(
        [product_over_rows(rows_full, grad_gate), product_over_rows(rows_full, grad_up)]
    )
    grad_rows = product_over_cols(grad_gate, weight_in[0]) + product_over_cols(
        grad_up, weight_in[1]
    )
    return (grad_rows, grad_weight_in, grad_weight_out)


def slot_pick(weight, select_low):
    return to_low(product_over_cols(weight, select_low))


def slot_weights(weight_qk, weight_vo, select_low):
    inner = HEADS * HEAD
    return (
        slot_pick(weight_qk[:, :inner], select_low),
        slot_pick(weight_qk[:, inner:], select_low),
        slot_pick(weight_vo[:, :inner], select_low),
        slot_pick(weight_vo[:, inner:], select_low),
    )


def project_three(rows_full, slots):
    return (
        to_low(product(rows_full, slots[0])),
        to_low(product(rows_full, slots[1])),
        to_low(product(rows_full, slots[2])),
    )


def three_back(rows_full, slots, grad_query, grad_keys, grad_values):
    grad_rows = (
        product_over_cols(grad_query, slots[0])
        + product_over_cols(grad_keys, slots[1])
        + product_over_cols(grad_values, slots[2])
    )
    return (
        grad_rows,
        product_over_rows(rows_full, grad_query),
        product_over_rows(rows_full, grad_keys),
        product_over_rows(rows_full, grad_values),
    )


def on_device(
    enc_x,
    dec_x,
    dec_cot,
    item_count,
    enc_mask,
    dec_mask,
    enc_buckets,
    dec_buckets,
    gains,
    tables,
    attn_qk,
    attn_vo,
    ff_in,
    ff_out,
):
    select, head_pick = tables_for(lax.axis_index("tensor"))
    select_stack = jnp.stack([tables_for(place)[0] for place in range(lax.axis_size("tensor"))])
    select_low = to_low(select)
    enc_slots = slot_weights(attn_qk[0], attn_vo[0], select_low)
    self_slots = slot_weights(attn_qk[1], attn_vo[1], select_low)
    cross_slots = slot_weights(attn_qk[2], attn_vo[2], select_low)
    enc_total = enc_mask.shape[0]
    dec_total = dec_mask.shape[0]
    groups = item_count[0]
    enc_item = jnp.arange(enc_total) // (enc_total // groups)
    dec_item = jnp.arange(dec_total) // (dec_total // groups)
    enc_live = enc_mask == 1
    dec_live = dec_mask == 1
    enc_terms, enc_onehot = offset_bias(enc_buckets, jnp.dot(tables[0], head_pick, precision=HIGH))
    self_terms, self_onehot = offset_bias(
        dec_buckets, jnp.dot(tables[1], head_pick, precision=HIGH)
    )
    enc_extra = make_extra(enc_item, enc_item, enc_live, False)
    self_extra = make_extra(dec_item, dec_item, dec_live, True)
    cross_extra = make_extra(dec_item, enc_item, enc_live, False)
    enc_start = enc_x.astype(jnp.float32)
    enc_attn_in = gather_rows(to_low(norm_gain(enc_start, gains[0])))
    queries, keys, values = project_three(enc_attn_in, enc_slots)
    partial_value, enc_attn_saved = attn_core(
        queries, keys, values, enc_slots[3], enc_extra, enc_spread, enc_terms
    )
    enc_mid = enc_start + reduce_rows(partial_value)
    enc_ff_in = gather_rows(to_low(norm_gain(enc_mid, gains[1])))
    partial_value, enc_ff_saved = ff_forward(enc_ff_in, ff_in[0], ff_out[0])
    enc_end = enc_mid + reduce_rows(partial_value)
    memory = to_low(norm_gain(enc_end, gains[2]))
    memory_all = lax.all_gather(memory, "tensor", axis=0, tiled=True)
    cross_keys = to_low(product(memory_all, cross_slots[1]))
    cross_values = to_low(product(memory_all, cross_slots[2]))
    dec_start = dec_x.astype(jnp.float32)
    self_in = gather_rows(to_low(norm_gain(dec_start, gains[3])))
    queries, keys, values = project_three(self_in, self_slots)
    partial_value, self_saved = attn_core(
        queries, keys, values, self_slots[3], self_extra, dec_spread, self_terms
    )
    dec_one = dec_start + reduce_rows(partial_value)
    cross_in = gather_rows(to_low(norm_gain(dec_one, gains[4])))
    partial_value, cross_saved = attn_core(
        to_low(product(cross_in, cross_slots[0])),
        cross_keys,
        cross_values,
        cross_slots[3],
        cross_extra,
        None,
        None,
    )
    dec_two = dec_one + reduce_rows(partial_value)
    dec_ff_in = gather_rows(to_low(norm_gain(dec_two, gains[5])))
    partial_value, dec_ff_saved = ff_forward(dec_ff_in, ff_in[1], ff_out[1])
    dec_out = (dec_two + reduce_rows(partial_value)).astype(jnp.bfloat16)
    residual = dec_cot.astype(jnp.float32)
    grad_full = gather_grads(to_low(residual))
    grad_rows, dec_ff_grad_in, dec_ff_grad_out = ff_back(
        grad_full, dec_ff_in, dec_ff_saved, ff_in[1], ff_out[1]
    )
    grad_rows, gain_five = norm_back(dec_two, gains[5], reduce_grads(grad_rows))
    residual = residual + grad_rows
    grad_full = gather_grads(to_low(residual))
    grad_query, grad_keys, grad_values, cross_grad_out, unused = attn_core_back(
        grad_full, cross_saved, cross_slots[3], cross_extra, None, None
    )
    cross_grad_query = product_over_rows(cross_in, grad_query)
    grad_rows, gain_four = norm_back(
        dec_one, gains[4], reduce_grads(product_over_cols(grad_query, cross_slots[0]))
    )
    memory_terms = product_over_cols(grad_keys, cross_slots[1]) + product_over_cols(
        grad_values, cross_slots[2]
    )
    memory_grad = lax.psum_scatter(memory_terms, "tensor", scatter_dimension=0, tiled=True)
    cross_grad_keys = product_over_rows(memory_all, grad_keys)
    cross_grad_values = product_over_rows(memory_all, grad_values)
    residual = residual + grad_rows
    grad_full = gather_grads(to_low(residual))
    grad_query, grad_keys, grad_values, self_grad_out, self_offsets = attn_core_back(
        grad_full, self_saved, self_slots[3], self_extra, dec_spread, self_terms
    )
    grad_rows, self_grad_query, self_grad_keys, self_grad_values = three_back(
        self_in, self_slots, grad_query, grad_keys, grad_values
    )
    grad_rows, gain_three = norm_back(dec_start, gains[3], reduce_grads(grad_rows))
    dec_grad = residual + grad_rows
    self_qk = jnp.concatenate([self_grad_query, self_grad_keys], axis=1)
    self_vo = jnp.concatenate([self_grad_values, self_grad_out], axis=1)
    cross_qk = jnp.concatenate([cross_grad_query, cross_grad_keys], axis=1)
    cross_vo = jnp.concatenate([cross_grad_values, cross_grad_out], axis=1)
    residual, gain_two = norm_back(enc_end, gains[2], memory_grad)
    grad_full = gather_grads(to_low(residual))
    grad_rows, enc_ff_grad_in, enc_ff_grad_out = ff_back(
        grad_full, enc_ff_in, enc_ff_saved, ff_in[0], ff_out[0]
    )
    grad_rows, gain_one = norm_back(enc_mid, gains[1], reduce_grads(grad_rows))
    residual = residual + grad_rows
    grad_full = gather_grads(to_low(residual))
    grad_query, grad_keys, grad_values, enc_grad_out, enc_offsets = attn_core_back(
        grad_full, enc_attn_saved, enc_slots[3], enc_extra, enc_spread, enc_terms
    )
    grad_rows, enc_grad_query, enc_grad_keys, enc_grad_values = three_back(
        enc_attn_in, enc_slots, grad_query, grad_keys, grad_values
    )
    grad_rows, gain_zero = norm_back(enc_start, gains[0], reduce_grads(grad_rows))
    enc_grad = residual + grad_rows
    enc_qk = jnp.concatenate([enc_grad_query, enc_grad_keys], axis=1)
    enc_vo = jnp.concatenate([enc_grad_values, enc_grad_out], axis=1)
    qk_sum, vo_sum = attn_reduce(
        jnp.stack([enc_qk, self_qk, cross_qk]), jnp.stack([enc_vo, self_vo, cross_vo]), select_stack
    )
    ffin_all = jnp.stack([enc_ff_grad_in, dec_ff_grad_in])
    ffout_all = jnp.stack([enc_ff_grad_out, dec_ff_grad_out])
    ffin_sum, ffout_sum = (
        lax.psum_scatter(ffin_all, "dp", scatter_dimension=2, tiled=True),
        lax.psum_scatter(ffout_all, "dp", scatter_dimension=2, tiled=True),
    )
    enc_table_grad = jnp.dot(
        jnp.dot(enc_onehot.T, enc_offsets.T, precision=HIGH), head_pick.T, precision=HIGH
    )
    self_table_grad = jnp.dot(
        jnp.dot(self_onehot.T, self_offsets.T, precision=HIGH), head_pick.T, precision=HIGH
    )
    gains_local = jnp.stack([gain_zero, gain_one, gain_two, gain_three, gain_four, gain_five])
    tables_local = jnp.stack([enc_table_grad, self_table_grad])
    gains_sum, tables_sum = lax.psum((gains_local, tables_local), ("dp", "tensor"))
    return (dec_out, enc_grad, dec_grad, gains_sum, tables_sum, qk_sum, vo_sum, ffin_sum, ffout_sum)


def solution(mesh):
    return jax.shard_map(
        on_device,
        mesh=mesh,
        in_specs=(
            P(("dp", "tensor"), None),
            P(("dp", "tensor"), None),
            P(("dp", "tensor"), None),
            P("dp"),
            P("dp"),
            P("dp"),
            P(),
            P(),
            P(),
            P(),
            P(),
            P(),
            P(None, None, None, "tensor"),
            P(None, "tensor", None),
        ),
        out_specs=(
            P(("dp", "tensor"), None),
            P(("dp", "tensor"), None),
            P(("dp", "tensor"), None),
            P(),
            P(),
            P(None, "dp", None),
            P(None, "dp", None),
            P(None, None, "dp", "tensor"),
            P(None, "tensor", "dp"),
        ),
        check_vma=False,
    )
```

profile of v0, /device:TPU:0, one launch (start us, length us, event | category | flops | bytes accessed | tf_op | source)
XLA Modules:
  0.0 1353.8 jit_solution(4059028185335504949)
XLA Ops:
  23.3 9.6 reshape.777
  60.1 39.8 %reduce-scatter.18.cloned.1.call-done = f32[128,1472]{0,1:T(8,128)} async-done(((f32[512,1472]{0,1:T(8,128)}), f32[128,1472]{0,1:T(8,128)}) %reduce-scatter.18.cloned.1.call-update) | async-done | bytes 753680 | tf_op jit(solution)/shard_map/reduce_scatter | solution.py:54
  102.6 19.4 %all-gather.10.cloned.1.call-done = bf16[512,1472]{0,1:T(8,128)(2,1)} async-done(((bf16[128,1472]{0,1:T(8,128)(2,1)}), bf16[512,1472]{0,1:T(8,128)(2,1)}) %all-gather.10.cloned.1.call-update) | async-done | bytes 1507344 | tf_op jit(solution)/shard_map/all_gather | solution.py:50
  138.8 6.0 all_gather.39
  161.2 12.4 reduce-scatter.20.cloned.1.call-done
  184.0 14.7 %reduce-scatter.16.cloned.1.call-done = f32[24,1472]{1,0:T(8,128)} async-done(((f32[96,1472]{1,0:T(8,128)}), f32[24,1472]{1,0:T(8,128)}) %reduce-scatter.16.cloned.1.call-update) | async-done | bytes 141328 | tf_op jit(solution)/shard_map/reduce_scatter | solution.py:54
  209.1 11.1 all-gather.12.cloned.1.call-done
  228.4 6.6 all_gather.45
  238.8 11.8 reduce-scatter.22.cloned.1.call-done
  272.3 20.9 %reduce-scatter.26.cloned.1.call-done = f32[24,1472]{1,0:T(8,128)} async-done(((f32[96,1472]{1,0:T(8,128)}), f32[24,1472]{1,0:T(8,128)}) %reduce-scatter.26.cloned.1.call-update) | async-done | bytes 141328 | tf_op jit(solution)/shard_map/reduce_scatter | solution.py:62
  314.4 37.3 %reduce-scatter.28.cloned.1.call-done = f32[128,1472]{0,1:T(8,128)} async-done(((f32[512,1472]{0,1:T(8,128)}), f32[128,1472]{0,1:T(8,128)}) %reduce-scatter.28.cloned.1.call-update) | async-done | bytes 753680 | tf_op jit(solution)/shard_map/reduce_scatter | solution.py:410
  356.6 19.6 %all-gather.14.cloned.1.call-done = bf16[512,1472]{0,1:T(8,128)(2,1)} async-done(((bf16[128,1472]{0,1:T(8,128)(2,1)}), bf16[512,1472]{0,1:T(8,128)(2,1)}) %all-gather.14.cloned.1.call-update) | async-done | bytes 1507344 | tf_op jit(solution)/shard_map/all_gather | solution.py:58
  376.2 6.2 multiply_convert_fusion.1
  404.9 24.4 %reduce-scatter.30.cloned.1.call-done = f32[128,1472]{0,1:T(8,128)} async-done(((f32[512,1472]{0,1:T(8,128)}), f32[128,1472]{0,1:T(8,128)}) %reduce-scatter.30.cloned.1.call-update) | async-done | bytes 753680 | tf_op jit(solution)/shard_map/reduce_scatter | solution.py:62
  437.4 16.3 %reduce-scatter.34.cloned.1.call-done = f32[24,1472]{1,0:T(8,128)} async-done(((f32[96,1472]{1,0:T(8,128)}), f32[24,1472]{1,0:T(8,128)}) %reduce-scatter.34.cloned.1.call-update) | async-done | bytes 141328 | tf_op jit(solution)/shard_map/reduce_scatter | solution.py:62
  454.8 23.5 %reduce-scatter.24.cloned.1.call-done = f32[24,1472]{1,0:T(8,128)} async-done(((f32[96,1472]{1,0:T(8,128)}), f32[24,1472]{1,0:T(8,128)}) %reduce-scatter.24.cloned.1.call-update) | async-done | bytes 141328 | tf_op jit(solution)/shard_map/reduce_scatter | solution.py:54
  488.3 10.9 all-gather.16.cloned.1.call-done
  526.7 74.0 %reduce-scatter.40.cloned.1.call-done = f32[3,184,256]{2,1,0:T(8,128)} async-done(((f32[3,1472,256]{2,1,0:T(8,128)}), f32[3,184,256]{2,1,0:T(8,128)}) %reduce-scatter.40.cloned.1.call-update) | async-done | bytes 565264 | tf_op jit(solution)/shard_map/reduce_scatter | solution.py:85
  600.8 96.4 %reduce-scatter.38.cloned.1.call-done = f32[3,184,256]{2,1,0:T(8,128)} async-done(((f32[3,1472,256]{2,1,0:T(8,128)}), f32[3,184,256]{2,1,0:T(8,128)}) %reduce-scatter.38.cloned.1.call-update) | async-done | bytes 565264 | tf_op jit(solution)/shard_map/reduce_scatter | solution.py:84
  735.4 8.9 maximum_bitcast_fusion
  744.3 12.2 pad_maximum_fusion
  772.6 41.0 %all-reduce.9 = (f32[6,1472]{1,0:T(8,128)}, f32[2,32,6]{1,2,0:T(8,128)S(1)}) all-reduce(f32[6,1472]{1,0:T(8,128)S(1)} %stack.105, f32[2,32,6]{1,2,0:T(8,128)S(1)} %pad_maximum_fusion.4), channel_id=1, replica_groups=mesh['dp'=8,'tensor'=4] {'dp','tensor'}, use_global_device_ids=true, to_apply=%region_38.39 | all-reduce | flops 9216 | bytes 73728 | tf_op jit(solution)/shard_map/psum | solution.py:462
  838.3 158.6 %reduce-scatter.44.cloned.1.call-done = f32[2,896,184]{1,2,0:T(8,128)} async-done(((f32[2,896,1472]{1,2,0:T(8,128)}), f32[2,896,184]{1,2,0:T(8,128)}) %reduce-scatter.44.cloned.1.call-update) | async-done | bytes 1318928 | tf_op jit(solution)/shard_map/reduce_scatter | solution.py:452
  996.9 349.8 %reduce-scatter.42.cloned.1.call-done = f32[2,2,184,896]{3,2,1,0:T(8,128)} async-done(((f32[2,2,1472,896]{3,2,1,0:T(8,128)}), f32[2,2,184,896]{3,2,1,0:T(8,128)}) %reduce-scatter.42.cloned.1.call-update) | async-done | bytes 2637840 | tf_op jit(solution)/shard_map/reduce_scatter | solution.py:451
  (632 shorter events, 305.1 us)
Async XLA Ops:
  7.2 43.0 %all-gather.8.cloned.1.call-start = ((), (), s32[]{:S(2)}) async-start(), calls=%async_computation.16 | async-start | bytes 1884160 | tf_op jit(solution)/shard_map/all_gather | solution.py:50
  10.8 189.0 %copy-start.83 = (f32[1472]{0:T(1024)}, f32[1472]{0:T(1024)S(1)}, u32[]{:S(2)}) copy-start(f32[1472]{0:T(1024)S(1)} %get-tuple-element.235) | copy-start | bytes 17668
  12.8 87.1 %reduce-scatter.18.cloned.1.call-start = ((), (), s32[]{:S(2)}) async-start(), calls=%async_computation.17 | async-start | bytes 3768320 | tf_op jit(solution)/shard_map/reduce_scatter | solution.py:54
  60.0 61.9 %all-gather.10.cloned.1.call-start = ((), (), s32[]{:S(2)}) async-start(), calls=%async_computation.18 | async-start | bytes 1884160 | tf_op jit(solution)/shard_map/all_gather | solution.py:50
  102.3 71.3 %reduce-scatter.20.cloned.1.call-start = ((), (), s32[]{:S(2)}) async-start(), calls=%async_computation.19 | async-start | bytes 3768320 | tf_op jit(solution)/shard_map/reduce_scatter | solution.py:54
  136.4 62.3 %reduce-scatter.16.cloned.1.call-start = ((), (), s32[]{:S(2)}) async-start(), calls=%async_computation.15 | async-start | bytes 737280 | tf_op jit(solution)/shard_map/reduce_scatter | solution.py:54
  158.6 61.6 %all-gather.12.cloned.1.call-start = ((), (), s32[]{:S(2)}) async-start(), calls=%async_computation.20 | async-start | bytes 1884160 | tf_op jit(solution)/shard_map/all_gather | solution.py:368
  176.9 73.7 %reduce-scatter.22.cloned.1.call-start = ((), (), s32[]{:S(2)}) async-start(), calls=%async_computation.21 | async-start | bytes 737280 | tf_op jit(solution)/shard_map/reduce_scatter | solution.py:54
  228.4 64.8 %reduce-scatter.26.cloned.1.call-start = ((), (), s32[]{:S(2)}) async-start(), calls=%async_computation.23 | async-start | bytes 737280 | tf_op jit(solution)/shard_map/reduce_scatter | solution.py:62
  270.9 80.8 %reduce-scatter.28.cloned.1.call-start = ((), (), s32[]{:S(2)}) async-start(), calls=%async_computation.24 | async-start | bytes 3768320 | tf_op jit(solution)/shard_map/reduce_scatter | solution.py:410
  314.4 61.8 %all-gather.14.cloned.1.call-start = ((), (), s32[]{:S(2)}) async-start(), calls=%async_computation.25 | async-start | bytes 1884160 | tf_op jit(solution)/shard_map/all_gather | solution.py:58
  356.6 72.6 %reduce-scatter.30.cloned.1.call-start = ((), (), s32[]{:S(2)}) async-start(), calls=%async_computation.26 | async-start | bytes 3768320 | tf_op jit(solution)/shard_map/reduce_scatter | solution.py:62
  391.9 61.7 %reduce-scatter.34.cloned.1.call-start = ((), (), s32[]{:S(2)}) async-start(), calls=%async_computation.29 | async-start | bytes 737280 | tf_op jit(solution)/shard_map/reduce_scatter | solution.py:62
  395.3 83.0 %reduce-scatter.24.cloned.1.call-start = ((), (), s32[]{:S(2)}) async-start(), calls=%async_computation.22 | async-start | bytes 737280 | tf_op jit(solution)/shard_map/reduce_scatter | solution.py:54
  400.7 98.5 %all-gather.16.cloned.1.call-start = ((), (), s32[]{:S(2)}) async-start(), calls=%async_computation.27 | async-start | bytes 1884160 | tf_op jit(solution)/shard_map/all_gather | solution.py:58
  434.6 166.1 %reduce-scatter.40.cloned.1.call-start = ((), (), s32[]{:S(2)}) async-start(), calls=%async_computation.33 | async-start | bytes 5087232 | tf_op jit(solution)/shard_map/reduce_scatter | solution.py:85
  507.4 189.7 %reduce-scatter.38.cloned.1.call-start = ((), (), s32[]{:S(2)}) async-start(), calls=%async_computation.31 | async-start | bytes 5087232 | tf_op jit(solution)/shard_map/reduce_scatter | solution.py:84
  519.7 202.3 %reduce-scatter.36.cloned.1.call-start = ((), (), s32[]{:S(2)}) async-start(), calls=%async_computation.30 | async-start | bytes 737280 | tf_op jit(solution)/shard_map/reduce_scatter | solution.py:62
  522.4 248.4 %reduce-scatter.32.cloned.1.call-start = ((), (), s32[]{:S(2)}) async-start(), calls=%async_computation.28 | async-start | bytes 3768320 | tf_op jit(solution)/shard_map/reduce_scatter | solution.py:62
  526.6 170.8 %copy-start.63 = (bf16[96,896]{1,0:T(8,128)(2,1)S(1)}, bf16[96,896]{1,0:T(8,128)(2,1)}, u32[]{:S(2)}) copy-start(bf16[96,896]{1,0:T(8,128)(2,1)} %get-tuple-element.273) | copy-start | bytes 516100
  526.6 289.9 %all-gather.20.cloned.1.call-start = ((), (), s32[]{:S(2)}) async-start(), calls=%async_computation.34 | async-start | bytes 2826240 | tf_op jit(solution)/shard_map/all_gather | solution.py:89
  600.7 226.7 %all-gather.18.cloned.1.call-start = ((), (), s32[]{:S(2)}) async-start(), calls=%async_computation.32 | async-start | bytes 2826240 | tf_op jit(solution)/shard_map/all_gather | solution.py:88
  697.2 299.8 %reduce-scatter.44.cloned.1.call-start = ((), (), s32[]{:S(2)}) async-start(), calls=%async_computation.36 | async-start | bytes 11870208 | tf_op jit(solution)/shard_map/reduce_scatter | solution.py:452
  705.1 641.6 %reduce-scatter.42.cloned.1.call-start = ((), (), s32[]{:S(2)}) async-start(), calls=%async_computation.35 | async-start | bytes 23740416 | tf_op jit(solution)/shard_map/reduce_scatter | solution.py:451
  (173 other events, 1882.6 us)
Sparse Core Ops, SparseCore 0:
  13.0 22.1 all-gather.7
  60.2 39.7 reduce-scatter.17
  102.4 19.4 all-gather.9
  136.5 37.1 reduce-scatter.19
  176.6 22.0 reduce-scatter.15
  200.7 19.4 all-gather.11
  228.5 22.0 reduce-scatter.21
  271.1 22.0 reduce-scatter.25
  314.5 37.1 reduce-scatter.27
  356.7 19.4 all-gather.13
  392.1 37.1 reduce-scatter.29
  431.6 22.0 reduce-scatter.33
  456.2 22.0 reduce-scatter.23
  479.7 19.4 all-gather.15
  507.5 93.1 reduce-scatter.39
  604.2 92.8 reduce-scatter.37
  700.0 21.8 reduce-scatter.35
  724.4 37.1 reduce-scatter.31
  763.1 24.0 all-gather.19
  788.7 23.9 all-gather.17
  817.2 179.7 reduce-scatter.43
  1001.4 345.3 reduce-scatter.41
where the time goes:
time: 1360 us; the launch traced here: 1350 us
  waiting for transfers between devices  946 us (70%)
  matrix products  141 us (10%)
  local copies, waits for them, and re-layouts  86.7 us (6%)
  other arithmetic  84.2 us (6%)
  blocking collectives  77 us (6%)
  between operations  17.5 us (1%)
    reduce_scatter x1, waiting for transfers between devices, on_device(): lax.psum_scatter(ffin_all, 'dp', scatter_dimension=2, tiled=True)  350 us
    reduce_scatter x1, waiting for transfers between devices, on_device(): lax.psum_scatter(ffout_all, 'dp', scatter_dimension=2, tiled=True)  159 us
    reduce_scatter x5, waiting for transfers between devices, reduce_rows(): return lax.psum_scatter(rows, 'tensor', scatter_dimension=0, tiled=True)  102 us
    reduce_scatter x1, waiting for transfers between devices, attn_reduce(): lax.psum_scatter(qk_slots, 'dp', scatter_dimension=1, tiled=True)  96.4 us
    reduce_scatter x1, waiting for transfers between devices, attn_reduce(): lax.psum_scatter(vo_slots, 'dp', scatter_dimension=1, tiled=True)  74 us
    reduce_scatter x5, waiting for transfers between devices, reduce_grads(): return lax.psum_scatter(rows, 'tensor', scatter_dimension=0, tiled=True)  66.6 us
    dot_general x30, matrix products, product_over_cols(): lax.dot_general(left, right, (((1,), (1,)), ((), ())), preferred_element_...  57.4 us
    psum x1, blocking collectives, on_device(): lax.psum((gains_local, tables_local), ('dp', 'tensor'))  41 us
  transfers between devices with their start and end apart: 22, of which 18 were waited for; matrix products, arithmetic and copies ran while one was open for 15% of the time, Pallas kernels for 0%

commit v1 on v0

v1 whole, which is shorter than its diff:
```python
import jax
import jax.numpy as jnp
from jax import lax
from jax.sharding import PartitionSpec as P

HEADS = 6
HEAD = 64
INNER = HEADS * HEAD
BUCKETS = 32
EPSILON = 1e-06
MASKED = -1000000000.0
HIGH = lax.Precision.HIGHEST


def norm_gain(rows, gain):
    return rows * lax.rsqrt(jnp.mean(rows * rows, axis=-1, keepdims=True) + EPSILON) * gain


def norm_back(rows, gain, grad_rows):
    unused, pullback = jax.vjp(norm_gain, rows, gain)
    return pullback(grad_rows)


def ff_act(gate, up_proj):
    return jax.nn.gelu(gate, approximate=True) * up_proj


def to_low(value):
    return value.astype(jnp.bfloat16)


def product(left, right):
    return jnp.dot(left, right, preferred_element_type=jnp.float32)


def product_over_rows(left, right):
    return lax.dot_general(
        left, right, (((0,), (0,)), ((), ())), preferred_element_type=jnp.float32
    )


def product_over_cols(left, right):
    return lax.dot_general(
        left, right, (((1,), (1,)), ((), ())), preferred_element_type=jnp.float32
    )


def gather_t(rows):
    return lax.all_gather(rows, "tensor", axis=0, tiled=True)


def scatter_t(rows):
    return lax.psum_scatter(to_low(rows), "tensor", scatter_dimension=0, tiled=True).astype(
        jnp.float32
    )


def offset_bias(buckets, table):
    onehot = (buckets[:, None] == jnp.arange(BUCKETS)[None, :]).astype(jnp.float32)
    return (jnp.dot(onehot, table, precision=HIGH).T, onehot)


def toeplitz(offset_terms, start, block, columns):
    period = 2 * columns
    wrapped = jnp.concatenate(
        [
            offset_terms[:, columns - 1 :],
            jnp.zeros((HEADS, 1), jnp.float32),
            offset_terms[:, : columns - 1],
        ],
        axis=1,
    )
    doubled = jnp.concatenate([wrapped, wrapped], axis=1)
    shift = (period - start % period) % period
    rolled = lax.dynamic_slice_in_dim(doubled, shift, period, 1)
    tiled = jnp.tile(rolled, (1, block))[:, : block * (period - 1)]
    return tiled.reshape(HEADS, block, period - 1)[:, :, :columns]


def dec_spread(offset_terms, start, block, columns):
    whole = jnp.concatenate(
        [offset_terms[:, ::-1], jnp.broadcast_to(offset_terms[:, :1], (HEADS, columns - 1))], axis=1
    )
    return toeplitz(whole, start, block, columns)


def heads_of(matrix):
    return matrix.reshape(matrix.shape[0], HEADS, HEAD)


def attend(queries, key_values, bias, allowed):
    key_heads = heads_of(key_values[:, :INNER])
    value_heads = heads_of(key_values[:, INNER:])
    raw = jnp.einsum(
        "rhd,shd->hrs", heads_of(queries), key_heads, preferred_element_type=jnp.float32
    )
    if bias is not None:
        raw = raw + bias
    scores = jnp.where(allowed[None], raw, MASKED)
    weights = jax.nn.softmax(scores, axis=-1)
    mixed = jnp.einsum(
        "hrs,shd->rhd", to_low(weights), value_heads, preferred_element_type=jnp.float32
    )
    return to_low(mixed.reshape(queries.shape[0], INNER)), weights


def attend_back(queries, key_values, weights, grad_out):
    key_heads = heads_of(key_values[:, :INNER])
    value_heads = heads_of(key_values[:, INNER:])
    grad_heads = heads_of(grad_out)
    grad_weights = jnp.einsum(
        "rhd,shd->hrs", grad_heads, value_heads, preferred_element_type=jnp.float32
    )
    weighted = jnp.sum(weights * grad_weights, axis=-1, keepdims=True)
    grad_scores = to_low(weights * (grad_weights - weighted))
    grad_query = jnp.einsum(
        "hrs,shd->rhd", grad_scores, key_heads, preferred_element_type=jnp.float32
    )
    grad_keys = jnp.einsum(
        "hrs,rhd->shd", grad_scores, heads_of(queries), preferred_element_type=jnp.float32
    )
    grad_values = jnp.einsum(
        "hrs,rhd->shd", to_low(weights), grad_heads, preferred_element_type=jnp.float32
    )
    total = key_values.shape[0]
    grad_kv = jnp.concatenate(
        [grad_keys.reshape(total, INNER), grad_values.reshape(total, INNER)], axis=1
    )
    return to_low(grad_query.reshape(queries.shape[0], INNER)), grad_kv, grad_scores


def pair_of(rows, place, size):
    split = rows.reshape(rows.shape[0], size // 2, 2, rows.shape[1] // size)
    return lax.dynamic_index_in_dim(split, place, 2, keepdims=False).reshape(
        rows.shape[0], rows.shape[1] // 2
    )


def dp_sum(left, right):
    size = lax.axis_size("dp")
    place = lax.axis_index("dp")
    block = left.shape[1] // size
    low_bit = place % 2
    send = to_low(product_over_rows(pair_of(left, 1 - low_bit, size), right))
    keep = product_over_rows(pair_of(left, low_bit, size), right)
    other = lax.ppermute(send, "dp", [(i, i ^ 1) for i in range(size)])
    current = (keep + other).reshape(size // 2, block, right.shape[1])
    bit = 2
    while bit < size:
        current = current.reshape(current.shape[0] // 2, 2, block, right.shape[1])
        here = (place // bit) % 2
        mine = lax.dynamic_index_in_dim(current, here, 1, keepdims=False)
        send = to_low(lax.dynamic_index_in_dim(current, 1 - here, 1, keepdims=False))
        other = lax.ppermute(send, "dp", [(i, i ^ bit) for i in range(size)])
        current = mine + other
        bit *= 2
    return current.reshape(block, right.shape[1])


def ff_forward(rows_full, weight_in, weight_out):
    gate = product(rows_full, weight_in[0])
    up_proj = product(rows_full, weight_in[1])
    hidden = to_low(ff_act(gate, up_proj))
    return (product(hidden, weight_out), (gate, up_proj, hidden))


def ff_back(grad_full, saved, weight_in, weight_out):
    gate, up_proj, hidden = saved
    grad_hidden = product_over_cols(grad_full, weight_out)
    unused, pullback = jax.vjp(ff_act, gate, up_proj)
    grad_gate, grad_up = pullback(grad_hidden)
    grad_gate = to_low(grad_gate)
    grad_up = to_low(grad_up)
    grad_rows = product_over_cols(grad_gate, weight_in[0]) + product_over_cols(
        grad_up, weight_in[1]
    )
    return (grad_rows, grad_gate, grad_up)


def to_owner(pieces):
    stacked = jnp.stack(pieces)
    out = lax.all_to_all(stacked, "tensor", 0, 0, tiled=True)
    return out.reshape(out.shape[0] * out.shape[1], out.shape[2])


def on_device(
    enc_x, dec_x, dec_cot, item_count, enc_mask, dec_mask, enc_buckets, dec_buckets,
    gains, tables, attn_qk, attn_vo, ff_in, ff_out,
):
    tensor_id = lax.axis_index("tensor")
    enc_total, dec_total = enc_mask.shape[0], dec_mask.shape[0]
    enc_own, dec_own = enc_x.shape[0], dec_x.shape[0]
    count = item_count[0]
    enc_place = tensor_id * enc_own + jnp.arange(enc_own)
    dec_place = tensor_id * dec_own + jnp.arange(dec_own)
    enc_item = jnp.arange(enc_total) // (enc_total // count)
    dec_item = jnp.arange(dec_total) // (dec_total // count)
    enc_item_own = enc_place // (enc_total // count)
    dec_item_own = dec_place // (dec_total // count)
    enc_live = enc_mask == 1
    dec_live = dec_mask == 1
    enc_allowed = (enc_item_own[:, None] == enc_item[None, :]) & enc_live[None, :]
    self_allowed = (
        (dec_item_own[:, None] == dec_item[None, :])
        & dec_live[None, :]
        & (jnp.arange(dec_total)[None, :] <= dec_place[:, None])
    )
    cross_allowed = (dec_item_own[:, None] == enc_item[None, :]) & enc_live[None, :]
    enc_terms, enc_onehot = offset_bias(enc_buckets, tables[0])
    self_terms, self_onehot = offset_bias(dec_buckets, tables[1])

    def enc_bias_of(terms):
        return toeplitz(terms, tensor_id * enc_own, enc_own, enc_total)

    def self_bias_of(terms):
        return dec_spread(terms, tensor_id * dec_own, dec_own, dec_total)

    enc_bias, enc_bias_back = jax.vjp(enc_bias_of, enc_terms)
    self_bias, self_bias_back = jax.vjp(self_bias_of, self_terms)

    def project(rows, a):
        return to_low(product(rows, attn_qk[a][:, :INNER]))

    def project_kv(rows, a):
        return jnp.concatenate(
            [
                to_low(product(rows, attn_qk[a][:, INNER:])),
                to_low(product(rows, attn_vo[a][:, :INNER])),
            ],
            axis=1,
        )

    def out_weight(a):
        return attn_vo[a][:, INNER:]

    enc_start = enc_x.astype(jnp.float32)
    enc_h0 = to_low(norm_gain(enc_start, gains[0]))
    enc_q = project(enc_h0, 0)
    enc_kv = gather_t(project_kv(enc_h0, 0))
    enc_o, enc_p = attend(enc_q, enc_kv, enc_bias, enc_allowed)
    enc_mid = enc_start + product_over_cols(enc_o, out_weight(0))
    enc_h1 = gather_t(to_low(norm_gain(enc_mid, gains[1])))
    partial_value, enc_ff_saved = ff_forward(enc_h1, ff_in[0], ff_out[0])
    enc_end = enc_mid + scatter_t(partial_value)
    memory = to_low(norm_gain(enc_end, gains[2]))
    cross_kv = gather_t(project_kv(memory, 2))

    dec_start = dec_x.astype(jnp.float32)
    dec_hs = to_low(norm_gain(dec_start, gains[3]))
    self_q = project(dec_hs, 1)
    self_kv = gather_t(project_kv(dec_hs, 1))
    self_o, self_p = attend(self_q, self_kv, self_bias, self_allowed)
    dec_one = dec_start + product_over_cols(self_o, out_weight(1))
    dec_hc = to_low(norm_gain(dec_one, gains[4]))
    cross_q = project(dec_hc, 2)
    cross_o, cross_p = attend(cross_q, cross_kv, None, cross_allowed)
    dec_two = dec_one + product_over_cols(cross_o, out_weight(2))
    dec_hf = gather_t(to_low(norm_gain(dec_two, gains[5])))
    partial_value, dec_ff_saved = ff_forward(dec_hf, ff_in[1], ff_out[1])
    dec_out = (dec_two + scatter_t(partial_value)).astype(jnp.bfloat16)

    residual = dec_cot.astype(jnp.float32)
    dec_gy = gather_t(dec_cot)
    grad_rows, dec_gg, dec_gu = ff_back(dec_gy, dec_ff_saved, ff_in[1], ff_out[1])
    grad_rows, gain_five = norm_back(dec_two, gains[5], scatter_t(grad_rows))
    residual = residual + grad_rows
    cross_gy = to_low(residual)
    grad_o = to_low(product(cross_gy, out_weight(2)))
    cross_gq, grad_kv, unused = attend_back(cross_q, cross_kv, cross_p, grad_o)
    cross_gkv = to_low(scatter_t(grad_kv))
    grad_rows, gain_four = norm_back(
        dec_one, gains[4], product_over_cols(cross_gq, attn_qk[2][:, :INNER])
    )
    residual = residual + grad_rows

    def kv_back(grad_kv, a):
        return product_over_cols(grad_kv[:, :INNER], attn_qk[a][:, INNER:]) + product_over_cols(
            grad_kv[:, INNER:], attn_vo[a][:, :INNER]
        )

    memory_grad = kv_back(cross_gkv, 2)
    self_gy = to_low(residual)
    grad_o = to_low(product(self_gy, out_weight(1)))
    self_gq, grad_kv, self_gs = attend_back(self_q, self_kv, self_p, grad_o)
    self_gkv = to_low(scatter_t(grad_kv))
    grad_rows, gain_three = norm_back(
        dec_start,
        gains[3],
        product_over_cols(self_gq, attn_qk[1][:, :INNER]) + kv_back(self_gkv, 1),
    )
    dec_grad = residual + grad_rows

    residual, gain_two = norm_back(enc_end, gains[2], memory_grad)
    enc_gy = gather_t(to_low(residual))
    grad_rows, enc_gg, enc_gu = ff_back(enc_gy, enc_ff_saved, ff_in[0], ff_out[0])
    grad_rows, gain_one = norm_back(enc_mid, gains[1], scatter_t(grad_rows))
    residual = residual + grad_rows
    enc_ay = to_low(residual)
    grad_o = to_low(product(enc_ay, out_weight(0)))
    enc_gq, grad_kv, enc_gs = attend_back(enc_q, enc_kv, enc_p, grad_o)
    enc_gkv = to_low(scatter_t(grad_kv))
    grad_rows, gain_zero = norm_back(
        enc_start,
        gains[0],
        product_over_cols(enc_gq, attn_qk[0][:, :INNER]) + kv_back(enc_gkv, 0),
    )
    enc_grad = residual + grad_rows

    def attn_weights(query_rows, key_rows, grad_y, grad_q, grad_kv, mixed):
        rows = query_rows.shape[0]
        more = key_rows.shape[0] - rows

        def fill(value):
            return jnp.pad(value, ((0, more), (0, 0))) if more else value

        left = to_owner([fill(query_rows), key_rows, key_rows, fill(grad_y)])
        right = to_owner([fill(grad_q), grad_kv[:, :INNER], grad_kv[:, INNER:], fill(mixed)])
        return dp_sum(left, right)

    dec_ff = [
        dp_sum(dec_hf, dec_gg),
        dp_sum(dec_hf, dec_gu),
        dp_sum(dec_gy, dec_ff_saved[2]).T,
    ]
    cross_w = attn_weights(dec_hc, memory, cross_gy, cross_gq, cross_gkv, cross_o)
    self_w = attn_weights(dec_hs, dec_hs, self_gy, self_gq, self_gkv, self_o)
    enc_ff = [
        dp_sum(enc_h1, enc_gg),
        dp_sum(enc_h1, enc_gu),
        dp_sum(enc_gy, enc_ff_saved[2]).T,
    ]
    enc_w = attn_weights(enc_h0, enc_h0, enc_ay, enc_gq, enc_gkv, enc_o)
    ffin_sum = jnp.stack([jnp.stack(enc_ff[:2]), jnp.stack(dec_ff[:2])])
    ffout_sum = jnp.stack([enc_ff[2], dec_ff[2]])
    attn_all = lax.all_gather(
        to_low(jnp.stack([enc_w, self_w, cross_w])), "tensor", axis=2, tiled=True
    ).astype(jnp.float32)
    qk_sum = attn_all[:, :, : 2 * INNER]
    vo_sum = attn_all[:, :, 2 * INNER :]

    enc_offsets = enc_bias_back(enc_gs.astype(jnp.float32))[0]
    self_offsets = self_bias_back(self_gs.astype(jnp.float32))[0]
    tables_local = jnp.stack(
        [
            jnp.dot(enc_onehot.T, enc_offsets.T, precision=HIGH),
            jnp.dot(self_onehot.T, self_offsets.T, precision=HIGH),
        ]
    )
    gains_local = jnp.stack([gain_zero, gain_one, gain_two, gain_three, gain_four, gain_five])
    gains_sum, tables_sum = lax.psum((gains_local, tables_local), ("dp", "tensor"))
    return (dec_out, enc_grad, dec_grad, gains_sum, tables_sum, qk_sum, vo_sum, ffin_sum, ffout_sum)


def solution(mesh):
    rows = P(("dp", "tensor"), None)
    return jax.shard_map(
        on_device,
        mesh=mesh,
        in_specs=(
            rows, rows, rows, P("dp"), P("dp"), P("dp"), P(), P(), P(), P(), P(), P(),
            P(None, None, None, "tensor"), P(None, "tensor", None),
        ),
        out_specs=(
            rows, rows, rows, P(), P(), P(None, "dp", None), P(None, "dp", None),
            P(None, None, "dp", "tensor"), P(None, "tensor", "dp"),
        ),
        check_vma=False,
    )
```

time: 1360 us -> 670 us (0.49)
  waiting for transfers between devices: 946 us -> 130 us
  local copies, waits for them, and re-layouts: 86.7 us -> 167 us
  starting transfers between devices: 1.51 us -> 57.2 us
  other arithmetic: 84.2 us -> 63.4 us
    reduce_scatter x15 -> x7, waiting for transfers between devices: 885 us -> 14.4 us  [scatter_t(): lax.psum_scatter(to_low(rows), 'tensor', scatter_dimension=0, tiled=True)]
    ppermute x0 -> x27, waiting for transfers between devices: none -> 89.8 us  [the longest x9 49.6 us: dp_sum(): other = lax.ppermute(send, 'dp', [(i, i ^ 1) for i in range(size)])]
    all_gather x7 -> x3, waiting for transfers between devices: 60.9 us -> 10.5 us  [the longest x2 10.5 us: gather_t(): return lax.all_gather(rows, 'tensor', axis=0, tiled=True)]
    ppermute x0 -> x27, starting transfers between devices: none -> 33.3 us  [the longest x18 22.5 us: dp_sum(): other = lax.ppermute(send, 'dp', [(i, i ^ bit) for i in range(size)])]
    all_to_all x0 -> x6, starting transfers between devices: none -> 22.7 us  [to_owner(): out = lax.all_to_all(stacked, 'tensor', 0, 0, tiled=True)]
    convert_element_type x6 -> x32, local copies, waits for them, and re-layouts: 2.63 us -> 24.1 us  [to_low(): return value.astype(jnp.bfloat16)]
    dynamic_slice x0 -> x7, local copies, waits for them, and re-layouts: none -> 17.7 us  [pair_of(): lax.dynamic_index_in_dim(split, place, 2, keepdims=False)]
    another operation x15 -> x21, other arithmetic: 39.7 us -> 22.5 us  [the longest x10 13.3 us: to_owner(): stacked = jnp.stack(pieces)]
  transfers between devices with their start and end apart: 22 -> 43, of which waited for: 18 -> 16; matrix products, arithmetic and copies ran while one was open for 15% -> 39% of each run, Pallas kernels for 0% -> 0%
where the time goes in v1:
time: 670 us; the launch traced here: 658 us
  local copies, waits for them, and re-layouts  167 us (25%)
  matrix products  144 us (21%)
  waiting for transfers between devices  130 us (19%)
  blocking collectives  78.2 us (12%)
  other arithmetic  63.4 us (9%)
  starting transfers between devices  57.2 us (9%)
  between operations  17.9 us (3%)
    ppermute x9, waiting for transfers between devices, dp_sum(): other = lax.ppermute(send, 'dp', [(i, i ^ 1) for i in range(size)])  49.6 us
    dot_general x18, matrix products, product_over_cols(): lax.dot_general(left, right, (((1,), (1,)), ((), ())), preferred_element_...  43.8 us
    psum x1, blocking collectives, on_device(): lax.psum((gains_local, tables_local), ('dp', 'tensor'))  41 us
    ppermute x18, waiting for transfers between devices, dp_sum(): other = lax.ppermute(send, 'dp', [(i, i ^ bit) for i in range(size)])  40.2 us
    dot_general x18, matrix products, product_over_rows(): lax.dot_general(left, right, (((0,), (0,)), ((), ())), preferred_element_...  37.7 us
    all_gather x5, blocking collectives, gather_t(): return lax.all_gather(rows, 'tensor', axis=0, tiled=True)  37.2 us
    dot_general x18, matrix products, product(): return jnp.dot(left, right, preferred_element_type=jnp.float32)  31.9 us
    unnamed x366, local copies, waits for them, and re-layouts  29.3 us
  transfers between devices with their start and end apart: 43, of which 16 were waited for; matrix products, arithmetic and copies ran while one was open for 39% of the time, Pallas kernels for 0%

profile of v1, /device:TPU:0, one launch (start us, length us, event | category | flops | bytes accessed | tf_op | source)
XLA Modules:
  0.0 657.6 jit_solution(7816795079787937604)
XLA Ops:
  12.2 5.6 slice_bitcast_fusion.1
  27.8 10.2 %all_gather.25 = bf16[512,768]{1,0:T(8,128)(2,1)S(1)} all-gather(bf16[128,768]{1,0:T(8,128)(2,1)S(1)} %pad_maximum_fusion.10), channel_id=1, replica_groups=mesh['dp'=8,'tensor'=4] {'tensor'}, dimensions={0}, use_global_device_ids=true | all-gather | bytes 983040 | tf_op jit(solution)/shard_map/all_gather | solution.py:49
  45.2 6.2 reshape.714
  67.9 5.7 all_gather.24
  74.9 10.5 %all-gather.4.cloned.1.call-done = bf16[512,1472]{1,0:T(8,128)(2,1)} async-done(((bf16[128,1472]{1,0:T(8,128)(2,1)}), bf16[512,1472]{1,0:T(8,128)(2,1)}) %all-gather.4.cloned.1.call-update) | async-done | bytes 1507344 | tf_op jit(solution)/shard_map/all_gather | solution.py:49
  89.6 5.7 multiply_convert_fusion.1
  112.2 6.1 all_gather.29
  143.2 9.1 %all_gather.27 = bf16[512,768]{1,0:T(8,128)(2,1)S(1)} all-gather(bf16[128,768]{1,0:T(8,128)(2,1)S(1)} %pad_maximum_fusion.11), channel_id=1, replica_groups=mesh['dp'=8,'tensor'=4] {'tensor'}, dimensions={0}, use_global_device_ids=true | all-gather | bytes 983040 | tf_op jit(solution)/shard_map/all_gather | solution.py:49
  164.6 6.0 all_gather.28
  209.6 8.2 %reduce-scatter.26.cloned.1.call-done = bf16[24,1472]{1,0:T(8,128)(2,1)} async-done(((bf16[96,1472]{1,0:T(8,128)(2,1)}), bf16[24,1472]{1,0:T(8,128)(2,1)}) %reduce-scatter.26.cloned.1.call-update) | async-done | bytes 70672 | tf_op jit(solution)/shard_map/reduce_scatter | solution.py:53
  234.2 6.2 reduce-scatter.24.cloned.1.call-done
  311.5 5.9 collective-permute-done.3
  326.0 7.9 %copy.297 = bf16[4,128,1472]{1,0,2:T(4,128)(2,1)} copy(bf16[4,128,1472]{1,2,0:T(8,128)(2,1)S(1)} %all-to-all-done.4) | data formatting | bytes 3014656 | tf_op jit(solution)/shard_map/all_to_all | solution.py:182
  338.0 6.8 %collective-permute-done.4 = bf16[2,184,384]{2,1,0:T(8,128)(2,1)} collective-permute-done((bf16[2,184,384]{2,1,0:T(8,128)(2,1)}, bf16[2,184,384]{2,1,0:T(8,128)(2,1)}, u32[]{:S(2)}, u32[]{:S(2)}) %collective-permute-start.4) | collective-permute-done | bytes 282656 | tf_op jit(solution)/shard_map/ppermute | solution.py:154
  374.6 16.7 %collective-permute-done.20 = bf16[1,184,896]{2,1,0:T(8,128)(2,1)} collective-permute-done((bf16[1,184,896]{2,1,0:T(8,128)(2,1)}, bf16[1,184,896]{2,1,0:T(8,128)(2,1)}, u32[]{:S(2)}, u32[]{:S(2)}) %collective-permute-start.20) | collective-permute-done | bytes 329760 | tf_op jit(solution)/shard_map/ppermute | solution.py:154
  395.7 6.1 multiply_convert_fusion
  428.2 6.6 %collective-permute-done.8 = bf16[1,184,384]{2,1,0:T(8,128)(2,1)S(1)} collective-permute-done((bf16[1,184,384]{2,1,0:T(8,128)(2,1)S(1)}, bf16[1,184,384]{2,1,0:T(8,128)(2,1)S(1)}, u32[]{:S(2)}, u32[]{:S(2)}) %collective-permute-start.8) | collective-permute-done | bytes 141344 | tf_op jit(solution)/shard_map/ppermute | solution.py:154
  444.7 8.2 %collective-permute-done.12 = bf16[736,896]{1,0:T(8,128)(2,1)} collective-permute-done((bf16[736,896]{1,0:T(8,128)(2,1)}, bf16[736,896]{1,0:T(8,128)(2,1)}, u32[]{:S(2)}, u32[]{:S(2)}) %collective-permute-start.12) | collective-permute-done | bytes 1318944 | tf_op jit(solution)/shard_map/ppermute | solution.py:146
  486.8 20.9 %collective-permute-done.21 = bf16[736,896]{1,0:T(8,128)(2,1)} collective-permute-done((bf16[736,896]{1,0:T(8,128)(2,1)}, bf16[736,896]{1,0:T(8,128)(2,1)}, u32[]{:S(2)}, u32[]{:S(2)}) %collective-permute-start.21) | collective-permute-done | bytes 1318944 | tf_op jit(solution)/shard_map/ppermute | solution.py:146
  536.8 8.4 %all-to-all-done = bf16[4,128,1472]{1,2,0:T(8,128)(2,1)} async-done(((bf16[4,128,1472]{1,2,0:T(8,128)(2,1)}), bf16[4,128,1472]{1,2,0:T(8,128)(2,1)}, u32[]{:S(2)}, u32[]{:S(2)}) %all-to-all-start) | async-done | bytes 1507360 | tf_op jit(solution)/shard_map/all_to_all | solution.py:182
  553.1 6.6 %copy.289 = bf16[4,128,1472]{1,0,2:T(4,128)(2,1)S(1)} copy(bf16[4,128,1472]{1,2,0:T(8,128)(2,1)} %all-to-all-done) | data formatting | bytes 3014656 | tf_op jit(solution)/shard_map/all_to_all | solution.py:182
  569.2 11.2 %collective-permute-done = bf16[736,384]{1,0:T(8,128)(2,1)S(1)} collective-permute-done((bf16[736,384]{1,0:T(8,128)(2,1)S(1)}, bf16[736,384]{1,0:T(8,128)(2,1)S(1)}, u32[]{:S(2)}, u32[]{:S(2)}) %collective-permute-start) | collective-permute-done | bytes 565280 | tf_op jit(solution)/shard_map/ppermute | solution.py:146
  584.6 5.6 collective-permute-done.1
  605.4 41.0 %all-reduce.13 = (f32[6,1472]{1,0:T(8,128)}, f32[2,32,6]{1,2,0:T(8,128)S(1)}) all-reduce(f32[6,1472]{1,0:T(8,128)S(1)} %stack.118, f32[2,32,6]{1,2,0:T(8,128)S(1)} %pad_maximum_fusion.15), channel_id=1, replica_groups=mesh['dp'=8,'tensor'=4] {'dp','tensor'}, use_global_device_ids=true, to_apply=%region_34.35 | all-reduce | flops 9216 | bytes 73728 | tf_op jit(solution)/shard_map/psum | solution.py:350
  (735 shorter events, 408.4 us)
Async XLA Ops:
  7.2 78.2 %all-gather.4.cloned.1.call-start = ((), (), s32[]{:S(2)}) async-start(), calls=%async_computation.13 | async-start | bytes 1966080 | tf_op jit(solution)/shard_map/all_gather | solution.py:49
  64.7 74.4 %reduce-scatter.22.cloned.1.call-start = ((), (), s32[]{:S(2)}) async-start(), calls=%async_computation.19 | async-start | bytes 1966080 | tf_op jit(solution)/shard_map/reduce_scatter | solution.py:53
  101.7 116.0 %reduce-scatter.26.cloned.1.call-start = ((), (), s32[]{:S(2)}) async-start(), calls=%async_computation.21 | async-start | bytes 368640 | tf_op jit(solution)/shard_map/reduce_scatter | solution.py:53
  197.2 43.2 %reduce-scatter.24.cloned.1.call-start = ((), (), s32[]{:S(2)}) async-start(), calls=%async_computation.20 | async-start | bytes 368640 | tf_op jit(solution)/shard_map/reduce_scatter | solution.py:53
  197.2 106.4 %collective-permute-start.18 = (bf16[736,896]{1,0:T(8,128)(2,1)}, bf16[736,896]{1,0:T(8,128)(2,1)}, u32[]{:S(2)}, u32[]{:S(2)}) collective-permute-start(bf16[736,896]{1,0:T(8,128)(2,1)} %convolution_convert_fusion.3), channel_id=1, source_target_pairs={{0,4},{4,0},{8,12},{12,8},{16,20},{20,16},{24,28},{28,24},{1,5},{5... | collective-permute-start | bytes 3956744 | tf_op jit(solution)/shard_map/ppermute | solution.py:146
  200.6 107.4 %collective-permute-start.15 = (bf16[736,896]{1,0:T(8,128)(2,1)}, bf16[736,896]{1,0:T(8,128)(2,1)}, u32[]{:S(2)}, u32[]{:S(2)}) collective-permute-start(bf16[736,896]{1,0:T(8,128)(2,1)} %convolution_convert_fusion.4), channel_id=1, source_target_pairs={{0,4},{4,0},{8,12},{12,8},{16,20},{20,16},{24,28},{28,24},{1,5},{5... | collective-permute-start | bytes 3956744 | tf_op jit(solution)/shard_map/ppermute | solution.py:146
  203.7 117.4 %collective-permute-start.24 = (bf16[736,896]{1,0:T(8,128)(2,1)}, bf16[736,896]{1,0:T(8,128)(2,1)}, u32[]{:S(2)}, u32[]{:S(2)}) collective-permute-start(bf16[736,896]{1,0:T(8,128)(2,1)} %convolution_convert_fusion.1), channel_id=1, source_target_pairs={{0,4},{4,0},{8,12},{12,8},{16,20},{20,16},{24,28},{28,24},{1,5},{5... | collective-permute-start | bytes 3956744 | tf_op jit(solution)/shard_map/ppermute | solution.py:146
  209.4 63.7 %reduce-scatter.20.cloned.1.call-start = ((), (), s32[]{:S(2)}) async-start(), calls=%async_computation.17 | async-start | bytes 184320 | tf_op jit(solution)/shard_map/reduce_scatter | solution.py:53
  252.1 97.6 %reduce-scatter.16.cloned.1.call-start = ((), (), s32[]{:S(2)}) async-start(), calls=%async_computation.14 | async-start | bytes 983040 | tf_op jit(solution)/shard_map/reduce_scatter | solution.py:53
  300.3 95.3 %all-gather.6.cloned.1.call-start = ((), (), s32[]{:S(2)}) async-start(), calls=%async_computation.15 | async-start | bytes 1966080 | tf_op jit(solution)/shard_map/all_gather | solution.py:49
  306.6 48.1 %collective-permute-start.19 = (bf16[2,184,896]{2,1,0:T(8,128)(2,1)}, bf16[2,184,896]{2,1,0:T(8,128)(2,1)}, u32[]{:S(2)}, u32[]{:S(2)}) collective-permute-start(bf16[2,184,896]{2,1,0:T(8,128)(2,1)} %fusion.111), channel_id=1, source_target_pairs={{0,8},{4,12},{8,0},{12,4},{16,24},{20,28},{24,16},{28,20},{1,9},{5... | collective-permute-start | bytes 1978376 | tf_op jit(solution)/shard_map/ppermute | solution.py:154
  310.9 48.0 %collective-permute-start.16 = (bf16[2,184,896]{2,1,0:T(8,128)(2,1)}, bf16[2,184,896]{2,1,0:T(8,128)(2,1)}, u32[]{:S(2)}, u32[]{:S(2)}) collective-permute-start(bf16[2,184,896]{2,1,0:T(8,128)(2,1)} %fusion.110), channel_id=1, source_target_pairs={{0,8},{4,12},{8,0},{12,4},{16,24},{20,28},{24,16},{28,20},{1,9},{5... | collective-permute-start | bytes 1978376 | tf_op jit(solution)/shard_map/ppermute | solution.py:154
  325.5 37.9 %collective-permute-start.25 = (bf16[2,184,896]{2,1,0:T(8,128)(2,1)}, bf16[2,184,896]{2,1,0:T(8,128)(2,1)}, u32[]{:S(2)}, u32[]{:S(2)}) collective-permute-start(bf16[2,184,896]{2,1,0:T(8,128)(2,1)} %fusion.113), channel_id=1, source_target_pairs={{0,8},{4,12},{8,0},{12,4},{16,24},{20,28},{24,16},{28,20},{1,9},{5... | collective-permute-start | bytes 1978376 | tf_op jit(solution)/shard_map/ppermute | solution.py:154
  361.3 52.2 %collective-permute-start.17 = (bf16[1,184,896]{2,1,0:T(8,128)(2,1)}, bf16[1,184,896]{2,1,0:T(8,128)(2,1)}, u32[]{:S(2)}, u32[]{:S(2)}) collective-permute-start(bf16[1,184,896]{2,1,0:T(8,128)(2,1)} %dynamic-slice_convert_fusion.3), channel_id=1, source_target_pairs={{0,16},{4,20},{8,24},{12,28},{16,0},{20,4},{24,8},{28,12},{1,17},{... | collective-permute-start | bytes 989192 | tf_op jit(solution)/shard_map/ppermute | solution.py:154
  366.5 48.3 %collective-permute-start.26 = (bf16[1,184,896]{2,1,0:T(8,128)(2,1)}, bf16[1,184,896]{2,1,0:T(8,128)(2,1)}, u32[]{:S(2)}, u32[]{:S(2)}) collective-permute-start(bf16[1,184,896]{2,1,0:T(8,128)(2,1)} %dynamic-slice_convert_fusion), channel_id=1, source_target_pairs={{0,16},{4,20},{8,24},{12,28},{16,0},{20,4},{24,8},{28,12},{1,17},{... | collective-permute-start | bytes 989192 | tf_op jit(solution)/shard_map/ppermute | solution.py:154
  371.7 85.1 %reduce-scatter.28.cloned.1.call-start = ((), (), s32[]{:S(2)}) async-start(), calls=%async_computation.22 | async-start | bytes 1966080 | tf_op jit(solution)/shard_map/reduce_scatter | solution.py:53
  413.3 101.3 %reduce-scatter.18.cloned.1.call-start = ((), (), s32[]{:S(2)}) async-start(), calls=%async_computation.16 | async-start | bytes 983040 | tf_op jit(solution)/shard_map/reduce_scatter | solution.py:53
  437.5 43.7 %collective-permute-start.9 = (bf16[736,896]{1,0:T(8,128)(2,1)}, bf16[736,896]{1,0:T(8,128)(2,1)}, u32[]{:S(2)}, u32[]{:S(2)}) collective-permute-start(bf16[736,896]{1,0:T(8,128)(2,1)} %convolution_convert_fusion.6), channel_id=1, source_target_pairs={{0,4},{4,0},{8,12},{12,8},{16,20},{20,16},{24,28},{28,24},{1,5},{5... | collective-permute-start | bytes 3956744 | tf_op jit(solution)/shard_map/ppermute | solution.py:146
  444.2 63.6 %collective-permute-start.21 = (bf16[736,896]{1,0:T(8,128)(2,1)}, bf16[736,896]{1,0:T(8,128)(2,1)}, u32[]{:S(2)}, u32[]{:S(2)}) collective-permute-start(bf16[736,896]{1,0:T(8,128)(2,1)} %convolution_convert_fusion.2), channel_id=1, source_target_pairs={{0,4},{4,0},{8,12},{12,8},{16,20},{20,16},{24,28},{28,24},{1,5},{5... | collective-permute-start | bytes 3956744 | tf_op jit(solution)/shard_map/ppermute | solution.py:146
  475.8 49.9 %collective-permute-start.13 = (bf16[2,184,896]{2,1,0:T(8,128)(2,1)}, bf16[2,184,896]{2,1,0:T(8,128)(2,1)}, u32[]{:S(2)}, u32[]{:S(2)}) collective-permute-start(bf16[2,184,896]{2,1,0:T(8,128)(2,1)} %fusion.109), channel_id=1, source_target_pairs={{0,8},{4,12},{8,0},{12,4},{16,24},{20,28},{24,16},{28,20},{1,9},{5... | collective-permute-start | bytes 1978376 | tf_op jit(solution)/shard_map/ppermute | solution.py:154
  484.8 44.6 %collective-permute-start.10 = (bf16[2,184,896]{2,1,0:T(8,128)(2,1)}, bf16[2,184,896]{2,1,0:T(8,128)(2,1)}, u32[]{:S(2)}, u32[]{:S(2)}) collective-permute-start(bf16[2,184,896]{2,1,0:T(8,128)(2,1)} %fusion.108), channel_id=1, source_target_pairs={{0,8},{4,12},{8,0},{12,4},{16,24},{20,28},{24,16},{28,20},{1,9},{5... | collective-permute-start | bytes 1978376 | tf_op jit(solution)/shard_map/ppermute | solution.py:154
  511.0 38.3 %collective-permute-start.22 = (bf16[2,184,896]{2,1,0:T(8,128)(2,1)}, bf16[2,184,896]{2,1,0:T(8,128)(2,1)}, u32[]{:S(2)}, u32[]{:S(2)}) collective-permute-start(bf16[2,184,896]{2,1,0:T(8,128)(2,1)} %fusion.112), channel_id=1, source_target_pairs={{0,8},{4,12},{8,0},{12,4},{16,24},{20,28},{24,16},{28,20},{1,9},{5... | collective-permute-start | bytes 1978376 | tf_op jit(solution)/shard_map/ppermute | solution.py:154
  528.0 39.0 %collective-permute-start.14 = (bf16[1,184,896]{2,1,0:T(8,128)(2,1)}, bf16[1,184,896]{2,1,0:T(8,128)(2,1)}, u32[]{:S(2)}, u32[]{:S(2)}) collective-permute-start(bf16[1,184,896]{2,1,0:T(8,128)(2,1)} %dynamic-slice_convert_fusion.4), channel_id=1, source_target_pairs={{0,16},{4,20},{8,24},{12,28},{16,0},{20,4},{24,8},{28,12},{1,17},{... | collective-permute-start | bytes 989192 | tf_op jit(solution)/shard_map/ppermute | solution.py:154
  549.3 97.7 %all-gather.8.cloned.1.call-start = ((), (), s32[]{:S(2)}) async-start(), calls=%async_computation.18 | async-start | bytes 2119680 | tf_op jit(solution)/shard_map/all_gather | solution.py:335
  (199 other events, 1504.0 us)
Sparse Core Ops, SparseCore 0:
  64.8 20.5 all-gather.3
  101.9 28.1 reduce-scatter.21
  197.3 20.4 reduce-scatter.25
  220.1 20.2 reduce-scatter.23
  252.2 19.6 reduce-scatter.19
  274.5 24.0 reduce-scatter.15
  354.8 18.3 all-gather.5
  413.4 27.4 reduce-scatter.27
  473.6 23.0 reduce-scatter.17
  601.1 19.8 all-gather.7

commit v2 on v1

v2 whole, which is shorter than its diff:
```python
import functools

import jax
import jax.numpy as jnp
from jax import lax
from jax.experimental import pallas as pl
from jax.experimental.pallas import tpu as pltpu
from jax.sharding import PartitionSpec as P

HEADS = 6
HEAD = 64
INNER = HEADS * HEAD
PAIRS = HEADS // 2
PAIR = 2 * HEAD
BUCKETS = 32
EPSILON = 1e-06
MASKED = -1000000000.0
HIGH = lax.Precision.HIGHEST
F32 = jnp.float32
LOW = jnp.bfloat16
DEC_PAD = 32
VMEM_BYTES = 60 * 1024 * 1024
ROOT = 0.7978845608028654
CUBE = 0.044715


def to_low(value):
    return value.astype(LOW)


def dot(left, right):
    return jnp.dot(left, right, preferred_element_type=F32)


def dot_first(left, right):
    return lax.dot_general(left, right, (((0,), (0,)), ((), ())), preferred_element_type=F32)


def dot_last(left, right):
    return lax.dot_general(left, right, (((1,), (1,)), ((), ())), preferred_element_type=F32)


def norm_gain(rows, gain):
    return rows * lax.rsqrt(jnp.mean(rows * rows, axis=-1, keepdims=True) + EPSILON) * gain


def norm_back(rows, gain, grad_rows):
    scale = lax.rsqrt(jnp.mean(rows * rows, axis=-1, keepdims=True) + EPSILON)
    normed = rows * scale
    scaled = grad_rows * gain
    inner = jnp.mean(scaled * normed, axis=-1, keepdims=True)
    grad_gain = jnp.sum(grad_rows * normed, axis=0, keepdims=True)
    return scale * (scaled - normed * inner), grad_gain


def act_parts(gate, up_proj):
    square = gate * gate
    curve = jnp.tanh(ROOT * gate * (1.0 + CUBE * square))
    half = 0.5 * (1.0 + curve)
    slope = half + 0.5 * gate * (1.0 - curve * curve) * (ROOT * (1.0 + 3.0 * CUBE * square))
    return gate * half, up_proj * slope


def tiles(width, step=256):
    return [(start, min(start + step, width)) for start in range(0, width, step)]


class Peers:
    def __init__(self, send_sem, recv_sem):
        dp, tensor = lax.axis_index("dp"), lax.axis_index("tensor")
        chip, core = lax.div(tensor, 2), lax.rem(tensor, 2)
        self.dp = dp
        self.own = tensor
        self.sib = chip * 2 + (1 - core)
        self.far = (1 - chip) * 2 + core
        self.diag = (1 - chip) * 2 + (1 - core)
        self.send_sem, self.recv_sem = send_sem, recv_sem
        self.used = 0
        self.copies = []

    def greet(self):
        barrier = pltpu.get_barrier_semaphore()
        for peer in (self.sib, self.far):
            pl.semaphore_signal(
                barrier, inc=1, device_id=(self.dp, peer), device_id_type=pl.DeviceIdType.MESH
            )
        pl.semaphore_wait(barrier, 2)

    def send(self, source, target, peer):
        place = self.used
        self.used += 1
        copy = pltpu.make_async_remote_copy(
            src_ref=source,
            dst_ref=target,
            send_sem=self.send_sem.at[place],
            recv_sem=self.recv_sem.at[place],
            device_id=(self.dp, peer),
            device_id_type=pl.DeviceIdType.MESH,
        )
        copy.start()
        self.copies.append(copy)
        return copy

    def finish(self):
        for copy in self.copies:
            copy.wait_send()


class Gather:
    def __init__(self, peers, buf, near):
        self.peers, self.buf = peers, buf
        if near:
            self.slots = (0, 1, 2, 2, 3)
        else:
            self.slots = (peers.own, peers.own, peers.own, peers.far, peers.far)

    def start(self):
        own, at_sib, at_far, unused, unused = self.slots
        self.to_far = self.peers.send(self.buf.at[own], self.buf.at[at_far], self.peers.far)
        self.to_sib = self.peers.send(self.buf.at[own], self.buf.at[at_sib], self.peers.sib)

    def wait_near(self):
        self.to_sib.wait_recv()

    def relay(self):
        unused, unused, unused, far, far_at_sib = self.slots
        self.to_far.wait_recv()
        self.relayed = self.peers.send(
            self.buf.at[far], self.buf.at[far_at_sib], self.peers.sib
        )

    def wait_far(self):
        self.relayed.wait_recv()


def attend(queries, kv, bias_of, allowed, weights_out, mixed_out):
    rows = queries.shape[0]
    total = kv.shape[0] * kv.shape[1]
    first = lax.broadcasted_iota(jnp.int32, (rows, PAIR), 1) < HEAD
    for pair in range(PAIRS):
        lanes = slice(pair * PAIR, (pair + 1) * PAIR)
        keys = kv[:, :, lanes].reshape(total, PAIR)
        values = kv[:, :, INNER + pair * PAIR : INNER + (pair + 1) * PAIR].reshape(total, PAIR)
        both = queries[:, lanes].astype(F32)
        mixed = []
        for half in range(2):
            head = 2 * pair + half
            here = to_low(jnp.where(first if half == 0 else ~first, both, 0.0))
            scores = dot_last(here, keys)
            if bias_of is not None:
                scores = scores + bias_of(head)
            scores = jnp.where(allowed, scores, MASKED)
            shifted = jnp.exp(scores - jnp.max(scores, axis=-1, keepdims=True))
            weights = shifted / jnp.sum(shifted, axis=-1, keepdims=True)
            weights_out[head] = weights
            mixed.append(dot(to_low(weights), values))
        mixed_out[:, lanes] = to_low(jnp.where(first, mixed[0], mixed[1]))


def attend_back(queries, kv, weights_in, grad_out, grad_q_out, grad_kv_out, grad_s_out):
    rows = queries.shape[0]
    total = kv.shape[0] * kv.shape[1]
    block = kv.shape[1]
    first = lax.broadcasted_iota(jnp.int32, (rows, PAIR), 1) < HEAD
    first_key = lax.broadcasted_iota(jnp.int32, (total, PAIR), 1) < HEAD
    for pair in range(PAIRS):
        lanes = slice(pair * PAIR, (pair + 1) * PAIR)
        value_lanes = slice(INNER + pair * PAIR, INNER + (pair + 1) * PAIR)
        keys = kv[:, :, lanes].reshape(total, PAIR)
        values = kv[:, :, value_lanes].reshape(total, PAIR)
        query = queries[:, lanes]
        grad = grad_out[:, lanes]
        grad_wide = grad.astype(F32)
        grad_q, grad_k, grad_v = [], [], []
        for half in range(2):
            head = 2 * pair + half
            here = to_low(jnp.where(first if half == 0 else ~first, grad_wide, 0.0))
            weights = weights_in[head]
            grad_weights = dot_last(here, values)
            weighted = jnp.sum(weights * grad_weights, axis=-1, keepdims=True)
            grad_scores = to_low(weights * (grad_weights - weighted))
            if grad_s_out is not None:
                grad_s_out[head] = grad_scores
            grad_q.append(dot(grad_scores, keys))
            grad_k.append(dot_first(grad_scores, query))
            grad_v.append(dot_first(to_low(weights), grad))
        grad_q_out[:, lanes] = to_low(jnp.where(first, grad_q[0], grad_q[1]))
        grad_kv_out[:, :, lanes] = jnp.where(first_key, grad_k[0], grad_k[1]).reshape(
            4, block, PAIR
        )
        grad_kv_out[:, :, value_lanes] = jnp.where(first_key, grad_v[0], grad_v[1]).reshape(
            4, block, PAIR
        )


class Loads:
    def __init__(self, sems):
        self.sems, self.used = sems, 0

    def start(self, source, target):
        copy = pltpu.make_async_copy(source, target, self.sems.at[self.used])
        self.used += 1
        copy.start()
        return copy


def project_kv(rows, wqk, wvo, target):
    target[:, :INNER] = to_low(dot(rows, wqk[:, INNER:]))
    target[:, INNER:] = to_low(dot(rows, wvo[:, :INNER]))


def ff_up(rows, w_in, gelu_out, slope_out, hidden_out, slots):
    count, block = slots.stop - slots.start, gelu_out.shape[1]
    for low, high in tiles(gelu_out.shape[2]):
        gate = dot(rows, w_in[0, :, low:high])
        up_proj = dot(rows, w_in[1, :, low:high])
        gelu, slope = act_parts(gate, up_proj)
        shape = (count, block, high - low)
        gelu_out[slots, :, low:high] = gelu.reshape(shape)
        slope_out[slots, :, low:high] = slope.reshape(shape)
        hidden_out[slots, :, low:high] = to_low(gelu * up_proj).reshape(shape)


def reduce_far(peers, diag_part, far_part, send, recv):
    width = send.shape[2]
    for low, high in tiles(width):
        send[0, :, low:high] = to_low(diag_part(low, high))
    first = peers.send(send.at[0], recv.at[0], peers.sib)
    first.wait_recv()
    for low, high in tiles(width):
        send[2, :, low:high] = to_low(
            far_part(low, high) + recv[0, :, low:high].astype(F32)
        )
    return peers.send(send.at[2], recv.at[2], peers.far)


def ka_kernel(
    enc_x, dec_x, dec_cot, gains, enc_terms, enc_code, enc_item, self_mask, self_bias, dec_item,
    qk_all, vo_all, fi_all, fo_all,
    h0, enc_q, enc_kv, enc_p, enc_o, enc_mid, h1, enc_gelu, enc_slope, enc_hidden, enc_end, memory,
    cross_kv, hs, self_q, self_kv, self_p, self_o, dec_one, hc, cross_q, cross_p, cross_o, dec_two,
    hf, dec_gy, dec_gg, dec_gu, dec_hidden,
    wqk, wvo, wfi, wfo, part, send, recv, dec_gelu, dec_slope, send_sem, recv_sem, load_sem,
):
    peers = Peers(send_sem, recv_sem)
    loads = Loads(load_sem)
    get_qk, get_vo, get_fi, get_fo = {}, {}, {}, {}
    for a in (0, 1):
        get_qk[a] = loads.start(qk_all.at[a], wqk.at[a])
        get_vo[a] = loads.start(vo_all.at[a], wvo.at[a])
    get_fi[0] = loads.start(fi_all.at[0], wfi.at[0])
    get_fo[0] = loads.start(fo_all.at[0], wfo.at[0])
    get_qk[2] = loads.start(qk_all.at[2], wqk.at[2])
    get_vo[2] = loads.start(vo_all.at[2], wvo.at[2])
    get_fi[1] = loads.start(fi_all.at[1], wfi.at[1])
    get_fo[1] = loads.start(fo_all.at[1], wfo.at[1])
    peers.greet()

    normed = to_low(norm_gain(enc_x[...].astype(F32), gains[0:1]))
    h0[...] = normed
    get_qk[0].wait()
    get_vo[0].wait()
    project_kv(normed, wqk.at[0], wvo.at[0], enc_kv.at[peers.own])
    enc_gather = Gather(peers, enc_kv, False)
    enc_gather.start()
    normed_dec = to_low(norm_gain(dec_x[...].astype(F32), gains[3:4]))
    hs[...] = normed_dec
    get_qk[1].wait()
    get_vo[1].wait()
    project_kv(normed_dec, wqk.at[1], wvo.at[1], self_kv.at[peers.own])
    self_gather = Gather(peers, self_kv, False)
    self_gather.start()
    dec_gy[0] = dec_cot[...]
    gy_gather = Gather(peers, dec_gy, True)
    gy_gather.start()
    enc_q[...] = to_low(dot(normed, wqk[0, :, :INNER]))
    self_q[...] = to_low(dot(normed_dec, wqk[1, :, :INNER]))

    enc_gather.wait_near()
    enc_gather.relay()
    enc_allowed = enc_item[...] == enc_code[...]

    def enc_bias(head):
        own_rows, period = h0.shape[0], enc_terms.shape[1]
        spread = jnp.broadcast_to(enc_terms[head : head + 1, :], (own_rows, period))
        rolled = pltpu.roll(spread, 0, 1, stride=1, stride_axis=0)
        return rolled[:, : period // 2]

    enc_gather.wait_far()
    attend(enc_q[...], enc_kv, enc_bias, enc_allowed, enc_p, enc_o)
    for low, high in tiles(enc_mid.shape[1]):
        enc_mid[:, low:high] = enc_x[:, low:high].astype(F32) + dot_last(
            enc_o[...], wvo[0, low:high, INNER:]
        )
    h1[0] = to_low(norm_gain(enc_mid[...], gains[1:2]))
    h1_gather = Gather(peers, h1, True)
    h1_gather.start()

    self_gather.wait_near()
    self_gather.relay()
    gy_gather.wait_near()
    gy_gather.relay()
    self_gather.wait_far()
    gy_gather.wait_far()
    attend(
        self_q[...], self_kv, lambda head: self_bias[head], self_mask[...] > 0.5, self_p, self_o
    )
    for low, high in tiles(dec_one.shape[1]):
        dec_one[:, low:high] = dec_x[:, low:high].astype(F32) + dot_last(
            self_o[...], wvo[1, low:high, INNER:]
        )
    normed_dec = to_low(norm_gain(dec_one[...], gains[4:5]))
    hc[...] = normed_dec

    h1_gather.wait_near()
    get_fi[0].wait()
    get_fo[0].wait()
    block, width = h1.shape[1], h1.shape[2]

    def both(buf, slots):
        return buf[slots].reshape((slots.stop - slots.start) * block, buf.shape[2])

    near, away = slice(0, 2), slice(2, 4)
    ff_up(both(h1, near), wfi.at[0], enc_gelu, enc_slope, enc_hidden, near)
    h1_gather.relay()
    h1_gather.wait_far()
    ff_up(both(h1, away), wfi.at[0], enc_gelu, enc_slope, enc_hidden, away)
    hidden = both(enc_hidden, away)
    for low, high in tiles(width):
        value = dot_last(hidden, wfo[0, low:high, :])
        part[:, low:high] = value[:block]
        send[0, :, low:high] = to_low(value[block:])
    first = peers.send(send.at[0], recv.at[0], peers.sib)
    get_qk[2].wait()
    get_vo[2].wait()
    cross_q[...] = to_low(dot(hc[...], wqk[2, :, :INNER]))
    first.wait_recv()
    send[2] = to_low(part[...] + recv[0].astype(F32))
    second = peers.send(send.at[2], recv.at[2], peers.far)
    hidden = both(enc_hidden, near)
    for low, high in tiles(width):
        value = dot_last(hidden, wfo[0, low:high, :])
        part[:, low:high] = value[:block] + enc_mid[:, low:high]
        send[1, :, low:high] = to_low(value[block:])
    third = peers.send(send.at[1], recv.at[1], peers.sib)
    third.wait_recv()
    part[...] = part[...] + recv[1].astype(F32)
    second.wait_recv()
    ended = part[...] + recv[2].astype(F32)
    enc_end[...] = ended
    normed = to_low(norm_gain(ended, gains[2:3]))
    memory[...] = normed

    project_kv(normed, wqk.at[2], wvo.at[2], cross_kv.at[peers.own])
    cross_gather = Gather(peers, cross_kv, False)
    cross_gather.start()
    get_fi[1].wait()
    get_fo[1].wait()
    cross_allowed = dec_item[...] == enc_code[...]
    cross_gather.wait_near()
    cross_gather.relay()
    cross_gather.wait_far()
    attend(cross_q[...], cross_kv, None, cross_allowed, cross_p, cross_o)
    for low, high in tiles(dec_two.shape[1]):
        dec_two[:, low:high] = dec_one[:, low:high] + dot_last(
            cross_o[...], wvo[2, low:high, INNER:]
        )
    hf[0] = to_low(norm_gain(dec_two[...], gains[5:6]))
    hf_gather = Gather(peers, hf, True)
    hf_gather.start()

    rows = hf.shape[0] * hf.shape[1]
    hf_gather.wait_near()
    hf_gather.relay()
    grad_y = dec_gy[...].reshape(rows, width)
    hf_gather.wait_far()
    ff_up(hf[...].reshape(rows, width), wfi.at[1], dec_gelu, dec_slope, dec_hidden, slice(0, 4))
    for low, high in tiles(dec_gelu.shape[2]):
        grad_h = dot(grad_y, wfo[1, :, low:high]).reshape(4, hf.shape[1], high - low)
        dec_gg[:, :, low:high] = to_low(grad_h * dec_slope[:, :, low:high])
        dec_gu[:, :, low:high] = to_low(grad_h * dec_gelu[:, :, low:high])
    peers.finish()


def ka_call(enc_x, dec_x, dec_cot, gains, enc_terms, enc_code, enc_item, self_mask, self_bias,
            dec_item, attn_qk, attn_vo, ff_in, ff_out):
    rows, width = enc_x.shape
    dec_rows = dec_x.shape[0]
    units = ff_in.shape[3]
    total = enc_code.shape[1]
    kv_width = 2 * INNER
    shape = jax.ShapeDtypeStruct
    outs = [
        shape((rows, width), LOW), shape((rows, INNER), LOW), shape((4, rows, kv_width), LOW),
        shape((HEADS, rows, total), F32), shape((rows, INNER), LOW), shape((rows, width), F32),
        shape((4, rows, width), LOW), shape((4, rows, units), F32), shape((4, rows, units), F32),
        shape((4, rows, units), LOW), shape((rows, width), F32), shape((rows, width), LOW),
        shape((4, rows, kv_width), LOW),
        shape((dec_rows, width), LOW), shape((dec_rows, INNER), LOW),
        shape((4, dec_rows, kv_width), LOW), shape((HEADS, dec_rows, 4 * dec_rows), F32),
        shape((dec_rows, INNER), LOW), shape((dec_rows, width), F32),
        shape((dec_rows, width), LOW), shape((dec_rows, INNER), LOW),
        shape((HEADS, dec_rows, total), F32), shape((dec_rows, INNER), LOW),
        shape((dec_rows, width), F32),
        shape((4, dec_rows, width), LOW), shape((4, dec_rows, width), LOW),
        shape((4, dec_rows, units), LOW), shape((4, dec_rows, units), LOW),
        shape((4, dec_rows, units), LOW),
    ]
    vmem = pl.BlockSpec(memory_space=pltpu.VMEM)
    hbm = pl.BlockSpec(memory_space=pltpu.HBM)
    copies = 3 * 6 + 3
    return pl.pallas_call(
        ka_kernel,
        out_shape=outs,
        in_specs=[vmem] * 10 + [hbm] * 4,
        out_specs=[vmem] * len(outs),
        scratch_shapes=[
            pltpu.VMEM(attn_qk.shape, LOW), pltpu.VMEM(attn_vo.shape, LOW),
            pltpu.VMEM(ff_in.shape, LOW), pltpu.VMEM(ff_out.shape, LOW),
            pltpu.VMEM((rows, width), F32), pltpu.VMEM((3, rows, width), LOW),
            pltpu.VMEM((3, rows, width), LOW), pltpu.VMEM((4, dec_rows, units), F32),
            pltpu.VMEM((4, dec_rows, units), F32),
            pltpu.SemaphoreType.DMA((copies,)), pltpu.SemaphoreType.DMA((copies,)),
            pltpu.SemaphoreType.DMA((10,)),
        ],
        compiler_params=pltpu.CompilerParams(
            collective_id=0, has_side_effects=True, vmem_limit_bytes=VMEM_BYTES
        ),
        name="forward_chain",
    )(enc_x, dec_x, dec_cot, gains, enc_terms, enc_code, enc_item, self_mask, self_bias, dec_item,
      attn_qk, attn_vo, ff_in, ff_out)


def pad_rows(value, rows=DEC_PAD):
    return jnp.pad(value, ((0, rows - value.shape[0]), (0, 0)))


def prepare(item_count, enc_mask, dec_mask, enc_buckets, dec_buckets, tables, enc_own, dec_own):
    tensor_id = lax.axis_index("tensor")
    enc_total, dec_total = enc_mask.shape[0], dec_mask.shape[0]
    count = item_count[0]
    enc_len, dec_len = enc_total // count, dec_total // count
    enc_code = jnp.where(enc_mask == 1, jnp.arange(enc_total) // enc_len, -1)
    enc_item = (tensor_id * enc_own + jnp.arange(enc_own)) // enc_len
    slot = jnp.arange(4 * DEC_PAD)
    inside = slot % DEC_PAD
    place = slot // DEC_PAD * dec_own + inside
    real = inside < dec_own
    row = jnp.arange(DEC_PAD)
    row_real = row < dec_own
    row_place = tensor_id * dec_own + row
    dec_live = jnp.pad(dec_mask.reshape(4, dec_own), ((0, 0), (0, DEC_PAD - dec_own))).reshape(-1)
    key_item = jnp.where(real & (dec_live == 1), place // dec_len, -1)
    dec_item = jnp.where(row_real, row_place // dec_len, -2)
    self_mask = (
        (dec_item[:, None] == key_item[None, :]) & (place[None, :] <= row_place[:, None])
    ).astype(F32)
    onehot = (enc_buckets[:, None] == jnp.arange(BUCKETS)[None, :]).astype(F32)
    terms = jnp.dot(tables[0].T, onehot.T, precision=HIGH)
    terms = jnp.pad(terms, ((0, 2), (0, 1)))
    period = 2 * enc_total
    doubled = jnp.concatenate([terms, terms], axis=1)
    shift = (enc_total - 1 - tensor_id * enc_own + period) % period
    enc_terms = lax.dynamic_slice_in_dim(doubled, shift, period, 1)
    far_back = jnp.clip(row_place[:, None] - place[None, :], 0, dec_total - 1)
    far_back = (far_back[None] == jnp.arange(dec_total)[:, None, None]).astype(F32)
    far_back = far_back.reshape(dec_total, -1)
    dec_onehot = (dec_buckets[:, None] == jnp.arange(BUCKETS)[None, :]).astype(F32)
    dec_terms = jnp.dot(tables[1].T, dec_onehot.T, precision=HIGH)
    self_bias = jnp.dot(dec_terms, far_back, precision=HIGH).reshape(
        HEADS, DEC_PAD, 4 * DEC_PAD
    )
    return (
        enc_terms, enc_code.astype(F32)[None, :], enc_item.astype(F32)[:, None], self_mask,
        self_bias, dec_item.astype(F32)[:, None],
    ), (onehot, dec_onehot, far_back)


def kv_back(grad_kv, wqk, wvo, low, high):
    return dot_last(grad_kv[:, :INNER], wqk[low:high, INNER:]) + dot_last(
        grad_kv[:, INNER:], wvo[low:high, :INNER]
    )


class SumBlocks:
    def __init__(self, peers, buf, send, recv):
        self.peers, self.buf, self.send, self.recv = peers, buf, send, recv
        send[0] = to_low(buf[peers.diag])
        send[1] = to_low(buf[peers.sib])
        self.first = peers.send(send.at[0], recv.at[0], peers.sib)
        self.third = peers.send(send.at[1], recv.at[1], peers.sib)

    def cross(self):
        peers = self.peers
        self.first.wait_recv()
        self.send[2] = to_low(self.buf[peers.far] + self.recv[0].astype(F32))
        self.second = peers.send(self.send.at[2], self.recv.at[2], peers.far)

    def result(self):
        self.third.wait_recv()
        value = self.buf[self.peers.own] + self.recv[1].astype(F32)
        self.second.wait_recv()
        return value + self.recv[2].astype(F32)


class SumNear:
    def __init__(self, peers, part_of, block, total, send, recv):
        self.peers, self.total, self.send, self.recv = peers, total, send, recv
        for low, high in tiles(send.shape[2]):
            value = part_of(low, high)
            total[0, :, low:high] = value[:block]
            send[1, :, low:high] = to_low(value[block : 2 * block])
            total[1, :, low:high] = value[2 * block : 3 * block]
            send[0, :, low:high] = to_low(value[3 * block :])
        self.first = peers.send(send.at[0], recv.at[0], peers.sib)
        self.third = peers.send(send.at[1], recv.at[1], peers.sib)

    def cross(self):
        self.first.wait_recv()
        self.send[2] = to_low(self.total[1] + self.recv[0].astype(F32))
        self.second = self.peers.send(self.send.at[2], self.recv.at[2], self.peers.far)

    def result(self):
        self.third.wait_recv()
        value = self.total[0] + self.recv[1].astype(F32)
        self.second.wait_recv()
        return value + self.recv[2].astype(F32)


def kb_kernel(
    dec_gg, dec_gu, dec_hidden, dec_cot, dec_two, dec_one, gains, cross_q, cross_kv, cross_p,
    enc_end, enc_gelu, enc_slope, qk_all, vo_all, fi_all, fo_all,
    dec_out, cross_gy, cross_gq, cross_gkv, dec_one_grad, enc_end_grad, enc_gy, enc_gg, enc_gu,
    gains_grad,
    wqk, wvo, wfi, wfo, grad_kv, kv_send, kv_recv, row_total, row_send, row_recv, out_total,
    out_send, out_recv, send_sem, recv_sem, load_sem,
):
    peers = Peers(send_sem, recv_sem)
    loads = Loads(load_sem)
    get_fi = loads.start(fi_all.at[1], wfi)
    get_vo = loads.start(vo_all.at[2], wvo)
    get_qk = loads.start(qk_all.at[2], wqk)
    get_fo1 = loads.start(fo_all.at[1], wfo.at[1])
    get_fo0 = loads.start(fo_all.at[0], wfo.at[0])
    peers.greet()
    width = dec_two.shape[1]
    block = dec_two.shape[0]
    units = dec_gg.shape[2]
    gains_grad[...] = jnp.zeros_like(gains_grad)

    get_fi.wait()
    gate, up_proj = dec_gg[...].reshape(4 * block, units), dec_gu[...].reshape(4 * block, units)

    def grad_rows_part(low, high):
        return dot_last(gate, wfi[0, low:high, :]) + dot_last(up_proj, wfi[1, low:high, :])

    grad_rows = SumNear(peers, grad_rows_part, block, row_total, row_send, row_recv)
    grad_rows.cross()
    get_vo.wait()
    get_qk.wait()
    value, gain_row = norm_back(dec_two[...], gains[5:6], grad_rows.result())
    gains_grad[5:6] = gain_row
    residual = dec_cot[...].astype(F32) + value
    grad_y = to_low(residual)
    cross_gy[...] = grad_y

    grad_out = to_low(dot(grad_y, wvo[:, INNER:]))
    attend_back(cross_q[...], cross_kv, cross_p, grad_out, cross_gq, grad_kv, None)
    kv_sum = SumBlocks(peers, grad_kv, kv_send, kv_recv)
    kv_sum.cross()
    for low, high in tiles(width):
        row_total[0, :, low:high] = dot_last(cross_gq[...], wqk[low:high, :INNER])
    value, gain_row = norm_back(dec_one[...], gains[4:5], row_total[0])
    gains_grad[4:5] = gain_row
    dec_one_grad[...] = residual + value
    own_kv = to_low(kv_sum.result())
    cross_gkv[...] = own_kv
    for low, high in tiles(width):
        enc_end_grad[:, low:high] = kv_back(own_kv, wqk, wvo, low, high)
    value, gain_row = norm_back(enc_end[...], gains[2:3], enc_end_grad[...])
    gains_grad[2:3] = gain_row
    enc_end_grad[...] = value
    enc_gy[0] = to_low(value)
    gy_gather = Gather(peers, enc_gy, True)
    gy_gather.start()

    get_fo1.wait()
    hidden = dec_hidden[...].reshape(4 * block, units)
    out_sum = SumNear(
        peers, lambda low, high: dot_last(hidden, wfo[1, low:high, :]), block, out_total,
        out_send, out_recv,
    )

    get_fo0.wait()
    rows = enc_gy.shape[1]

    def gate_grads(slots):
        grad_y = enc_gy[slots].reshape(2 * rows, width)
        for low, high in tiles(units):
            grad_h = dot(grad_y, wfo[0, :, low:high]).reshape(2, rows, high - low)
            enc_gg[slots, :, low:high] = to_low(grad_h * enc_slope[slots, :, low:high])
            enc_gu[slots, :, low:high] = to_low(grad_h * enc_gelu[slots, :, low:high])

    gy_gather.wait_near()
    gate_grads(slice(0, 2))
    gy_gather.relay()
    out_sum.cross()
    gy_gather.wait_far()
    gate_grads(slice(2, 4))
    dec_out[...] = to_low(dec_two[...] + out_sum.result())
    peers.finish()


def kb_call(dec_gg, dec_gu, dec_hidden, dec_cot, dec_two, dec_one, gains, cross_q, cross_kv,
            cross_p, enc_end, enc_gelu, enc_slope, attn_qk, attn_vo, ff_in, ff_out):
    rows, width = enc_end.shape
    dec_rows = dec_two.shape[0]
    units = ff_in.shape[3]
    kv_width = 2 * INNER
    shape = jax.ShapeDtypeStruct
    outs = [
        shape((dec_rows, width), LOW), shape((dec_rows, width), LOW),
        shape((dec_rows, INNER), LOW), shape((rows, kv_width), LOW), shape((dec_rows, width), F32),
        shape((rows, width), F32), shape((4, rows, width), LOW), shape((4, rows, units), LOW),
        shape((4, rows, units), LOW), shape((8, width), F32),
    ]
    vmem = pl.BlockSpec(memory_space=pltpu.VMEM)
    hbm = pl.BlockSpec(memory_space=pltpu.HBM)
    copies = 3 * 3 + 3
    return pl.pallas_call(
        kb_kernel,
        out_shape=outs,
        in_specs=[vmem] * 13 + [hbm] * 4,
        out_specs=[vmem] * len(outs),
        scratch_shapes=[
            pltpu.VMEM(attn_qk.shape[1:], LOW), pltpu.VMEM(attn_vo.shape[1:], LOW),
            pltpu.VMEM(ff_in.shape[1:], LOW), pltpu.VMEM(ff_out.shape, LOW),
            pltpu.VMEM((4, rows, kv_width), F32), pltpu.VMEM((3, rows, kv_width), LOW),
            pltpu.VMEM((3, rows, kv_width), LOW), pltpu.VMEM((2, dec_rows, width), F32),
            pltpu.VMEM((3, dec_rows, width), LOW), pltpu.VMEM((3, dec_rows, width), LOW),
            pltpu.VMEM((2, dec_rows, width), F32), pltpu.VMEM((3, dec_rows, width), LOW),
            pltpu.VMEM((3, dec_rows, width), LOW),
            pltpu.SemaphoreType.DMA((copies,)), pltpu.SemaphoreType.DMA((copies,)),
            pltpu.SemaphoreType.DMA((5,)),
        ],
        compiler_params=pltpu.CompilerParams(
            collective_id=1, has_side_effects=True, vmem_limit_bytes=VMEM_BYTES
        ),
        name="middle_chain",
    )(dec_gg, dec_gu, dec_hidden, dec_cot, dec_two, dec_one, gains, cross_q, cross_kv, cross_p,
      enc_end, enc_gelu, enc_slope, attn_qk, attn_vo, ff_in, ff_out)


def kc_kernel(
    enc_gg, enc_gu, enc_end_grad, enc_mid, enc_x, gains, enc_q, enc_kv, enc_p, dec_one_grad, dec_x,
    self_q, self_kv, self_p, qk_all, vo_all, fi_all,
    enc_grad, enc_ay, enc_gq, enc_gkv, enc_offsets, dec_grad, self_gy, self_gq, self_gkv, self_gs,
    gains_grad,
    wqk, wvo, wfi, enc_gs, part, send, recv, enc_gkv_full, kv_send, kv_recv, self_gkv_full,
    self_send, self_recv, send_sem, recv_sem, load_sem,
):
    peers = Peers(send_sem, recv_sem)
    loads = Loads(load_sem)
    get_fi = loads.start(fi_all.at[0], wfi)
    get_vo1 = loads.start(vo_all.at[1], wvo.at[1])
    get_qk1 = loads.start(qk_all.at[1], wqk.at[1])
    get_vo0 = loads.start(vo_all.at[0], wvo.at[0])
    get_qk0 = loads.start(qk_all.at[0], wqk.at[0])
    peers.greet()
    rows, width = enc_mid.shape
    units = enc_gg.shape[2]
    gains_grad[...] = jnp.zeros_like(gains_grad)

    get_fi.wait()

    def grad_part(slots, low, high):
        gate = enc_gg[slots].reshape(2 * rows, units)
        up_proj = enc_gu[slots].reshape(2 * rows, units)
        return dot_last(gate, wfi[0, low:high, :]) + dot_last(up_proj, wfi[1, low:high, :])

    for low, high in tiles(width):
        value = grad_part(slice(2, 4), low, high)
        part[:, low:high] = value[:rows]
        send[0, :, low:high] = to_low(value[rows:])
    first = peers.send(send.at[0], recv.at[0], peers.sib)
    get_vo1.wait()
    residual_dec = dec_one_grad[...]
    grad_y = to_low(residual_dec)
    self_gy[...] = grad_y
    grad_out_dec = to_low(dot(grad_y, wvo[1, :, INNER:]))
    first.wait_recv()
    send[2] = to_low(part[...] + recv[0].astype(F32))
    second = peers.send(send.at[2], recv.at[2], peers.far)
    for low, high in tiles(width):
        value = grad_part(slice(0, 2), low, high)
        part[:, low:high] = value[:rows]
        send[1, :, low:high] = to_low(value[rows:])
    third = peers.send(send.at[1], recv.at[1], peers.sib)

    attend_back(self_q[...], self_kv, self_p, grad_out_dec, self_gq, self_gkv_full, self_gs)
    self_sum = SumBlocks(peers, self_gkv_full, self_send, self_recv)
    self_sum.cross()

    third.wait_recv()
    part[...] = part[...] + recv[1].astype(F32)
    second.wait_recv()
    get_vo0.wait()
    value, gain_row = norm_back(enc_mid[...], gains[1:2], part[...] + recv[2].astype(F32))
    gains_grad[1:2] = gain_row
    residual = enc_end_grad[...] + value
    grad_y = to_low(residual)
    enc_ay[...] = grad_y
    enc_grad[...] = residual

    grad_out = to_low(dot(grad_y, wvo[0, :, INNER:]))
    attend_back(enc_q[...], enc_kv, enc_p, grad_out, enc_gq, enc_gkv_full, enc_gs)
    enc_sum = SumBlocks(peers, enc_gkv_full, kv_send, kv_recv)
    get_qk0.wait()
    for low, high in tiles(width):
        part[:, low:high] = dot_last(enc_gq[...], wqk[0, low:high, :INNER])
    enc_sum.cross()

    get_qk1.wait()
    own_kv = to_low(self_sum.result())
    self_gkv[...] = own_kv
    for low, high in tiles(width):
        dec_grad[:, low:high] = dot_last(self_gq[...], wqk[1, low:high, :INNER]) + kv_back(
            own_kv, wqk.at[1], wvo.at[1], low, high
        )
    value, gain_row = norm_back(dec_x[...].astype(F32), gains[3:4], dec_grad[...])
    gains_grad[3:4] = gain_row
    dec_grad[...] = residual_dec + value

    turn = lax.broadcasted_iota(jnp.int32, (rows, rows), 0) + lax.broadcasted_iota(
        jnp.int32, (rows, rows), 1
    )
    turn = jnp.where(turn == rows - 1, 1.0, 0.0).astype(LOW)
    enc_offsets[...] = jnp.zeros_like(enc_offsets)
    for head in range(HEADS):
        turned = dot(turn, enc_gs[head])
        spread = jnp.concatenate([turned, jnp.zeros((rows, rows), F32)], axis=1)
        spread = pltpu.roll(spread, 0, 1, stride=1, stride_axis=0)
        enc_offsets[head : head + 1, :] = jnp.sum(spread, axis=0, keepdims=True)

    own_kv = to_low(enc_sum.result())
    enc_gkv[...] = own_kv
    for low, high in tiles(width):
        part[:, low:high] += kv_back(own_kv, wqk.at[0], wvo.at[0], low, high)
    value, gain_row = norm_back(enc_x[...].astype(F32), gains[0:1], part[...])
    gains_grad[0:1] = gain_row
    enc_grad[...] += value
    peers.finish()


def kc_call(enc_gg, enc_gu, enc_end_grad, enc_mid, enc_x, gains, enc_q, enc_kv, enc_p,
            dec_one_grad, dec_x, self_q, self_kv, self_p, attn_qk, attn_vo, ff_in):
    rows, width = enc_x.shape
    dec_rows = dec_x.shape[0]
    units = ff_in.shape[3]
    kv_width = 2 * INNER
    total = 4 * rows
    shape = jax.ShapeDtypeStruct
    outs = [
        shape((rows, width), F32), shape((rows, width), LOW), shape((rows, INNER), LOW),
        shape((rows, kv_width), LOW), shape((8, total + rows), F32),
        shape((dec_rows, width), F32), shape((dec_rows, width), LOW),
        shape((dec_rows, INNER), LOW), shape((dec_rows, kv_width), LOW),
        shape((HEADS, dec_rows, 4 * dec_rows), LOW), shape((8, width), F32),
    ]
    vmem = pl.BlockSpec(memory_space=pltpu.VMEM)
    hbm = pl.BlockSpec(memory_space=pltpu.HBM)
    copies = 3 * 3
    return pl.pallas_call(
        kc_kernel,
        out_shape=outs,
        in_specs=[vmem] * 14 + [hbm] * 3,
        out_specs=[vmem] * len(outs),
        scratch_shapes=[
            pltpu.VMEM((2,) + attn_qk.shape[1:], LOW), pltpu.VMEM((2,) + attn_vo.shape[1:], LOW),
            pltpu.VMEM(ff_in.shape[1:], LOW), pltpu.VMEM((HEADS, rows, total), LOW),
            pltpu.VMEM((rows, width), F32), pltpu.VMEM((3, rows, width), LOW),
            pltpu.VMEM((3, rows, width), LOW),
            pltpu.VMEM((4, rows, kv_width), F32), pltpu.VMEM((3, rows, kv_width), LOW),
            pltpu.VMEM((3, rows, kv_width), LOW),
            pltpu.VMEM((4, dec_rows, kv_width), F32), pltpu.VMEM((3, dec_rows, kv_width), LOW),
            pltpu.VMEM((3, dec_rows, kv_width), LOW),
            pltpu.SemaphoreType.DMA((copies,)), pltpu.SemaphoreType.DMA((copies,)),
            pltpu.SemaphoreType.DMA((5,)),
        ],
        compiler_params=pltpu.CompilerParams(
            collective_id=2, has_side_effects=True, vmem_limit_bytes=VMEM_BYTES
        ),
        name="last_chain",
    )(enc_gg, enc_gu, enc_end_grad, enc_mid, enc_x, gains, enc_q, enc_kv, enc_p, dec_one_grad,
      dec_x, self_q, self_kv, self_p, attn_qk, attn_vo, ff_in)


def pair_of(rows, place, size):
    split = rows.reshape(rows.shape[0], size // 2, 2, rows.shape[1] // size)
    return lax.dynamic_index_in_dim(split, place, 2, keepdims=False).reshape(
        rows.shape[0], rows.shape[1] // 2
    )


def dp_sum(left, right):
    size = lax.axis_size("dp")
    place = lax.axis_index("dp")
    block = left.shape[1] // size
    low_bit = place % 2
    send = to_low(dot_first(pair_of(left, 1 - low_bit, size), right))
    keep = dot_first(pair_of(left, low_bit, size), right)
    other = lax.ppermute(send, "dp", [(i, i ^ 1) for i in range(size)])
    current = (keep + other).reshape(size // 2, block, right.shape[1])
    bit = 2
    while bit < size:
        current = current.reshape(current.shape[0] // 2, 2, block, right.shape[1])
        here = (place // bit) % 2
        mine = lax.dynamic_index_in_dim(current, here, 1, keepdims=False)
        send = to_low(lax.dynamic_index_in_dim(current, 1 - here, 1, keepdims=False))
        other = lax.ppermute(send, "dp", [(i, i ^ bit) for i in range(size)])
        current = mine + other
        bit *= 2
    return current.reshape(block, right.shape[1])


def to_owner(pieces):
    out = lax.all_to_all(jnp.stack(pieces), "tensor", 0, 0, tiled=True)
    return out.reshape(out.shape[0] * out.shape[1], out.shape[2])


def attn_weights(query_rows, key_rows, grad_y, grad_q, grad_kv, mixed):
    more = key_rows.shape[0] - query_rows.shape[0]

    def fill(value):
        return jnp.pad(value, ((0, more), (0, 0))) if more else value

    left = to_owner([fill(query_rows), key_rows, key_rows, fill(grad_y)])
    right = to_owner([fill(grad_q), grad_kv[:, :INNER], grad_kv[:, INNER:], fill(mixed)])
    return dp_sum(left, right)


def flat(blocks):
    return blocks.reshape(blocks.shape[0] * blocks.shape[1], blocks.shape[2])


def on_device(
    enc_x, dec_x, dec_cot, item_count, enc_mask, dec_mask, enc_buckets, dec_buckets,
    gains, tables, attn_qk, attn_vo, ff_in, ff_out,
):
    tensor_id = lax.axis_index("tensor")
    enc_own, dec_own = enc_x.shape[0], dec_x.shape[0]
    enc_total = enc_mask.shape[0]
    small, (onehot, dec_onehot, far_back) = prepare(
        item_count, enc_mask, dec_mask, enc_buckets, dec_buckets, tables, enc_own, dec_own
    )
    ff_out_t = jnp.swapaxes(ff_out, 1, 2)
    dec_x, dec_cot = pad_rows(dec_x), pad_rows(dec_cot)
    (
        h0, enc_q, enc_kv, enc_p, enc_o, enc_mid, h1, enc_gelu, enc_slope, enc_hidden, enc_end,
        memory, cross_kv, hs, self_q, self_kv, self_p, self_o, dec_one, hc, cross_q, cross_p,
        cross_o, dec_two, hf, dec_gy, dec_gg, dec_gu, dec_hidden,
    ) = ka_call(enc_x, dec_x, dec_cot, gains, *small, attn_qk, attn_vo, ff_in, ff_out_t)
    dec_ff = [
        dp_sum(flat(hf), flat(dec_gg)),
        dp_sum(flat(hf), flat(dec_gu)),
        dp_sum(flat(dec_gy), flat(dec_hidden)).T,
    ]
    (
        dec_out, cross_gy, cross_gq, cross_gkv, dec_one_grad, enc_end_grad, enc_gy, enc_gg, enc_gu,
        gains_b,
    ) = kb_call(
        dec_gg, dec_gu, dec_hidden, dec_cot, dec_two, dec_one, gains, cross_q, cross_kv, cross_p,
        enc_end, enc_gelu, enc_slope, attn_qk, attn_vo, ff_in, ff_out_t,
    )
    enc_ff = [
        dp_sum(flat(h1), flat(enc_gg)),
        dp_sum(flat(h1), flat(enc_gu)),
        dp_sum(flat(enc_gy), flat(enc_hidden)).T,
    ]
    cross_w = attn_weights(hc, memory, cross_gy, cross_gq, cross_gkv, cross_o)
    (
        enc_grad, enc_ay, enc_gq, enc_gkv, enc_offsets, dec_grad, self_gy, self_gq, self_gkv,
        self_gs, gains_c,
    ) = kc_call(
        enc_gg, enc_gu, enc_end_grad, enc_mid, enc_x, gains, enc_q, enc_kv, enc_p, dec_one_grad,
        dec_x, self_q, self_kv, self_p, attn_qk, attn_vo, ff_in,
    )
    self_w = attn_weights(hs, hs, self_gy, self_gq, self_gkv, self_o)
    enc_w = attn_weights(h0, h0, enc_ay, enc_gq, enc_gkv, enc_o)
    ffin_sum = jnp.stack([jnp.stack(enc_ff[:2]), jnp.stack(dec_ff[:2])])
    ffout_sum = jnp.stack([enc_ff[2], dec_ff[2]])
    attn_all = lax.all_gather(
        to_low(jnp.stack([enc_w, self_w, cross_w])), "tensor", axis=2, tiled=True
    ).astype(F32)
    qk_sum = attn_all[:, :, : 2 * INNER]
    vo_sum = attn_all[:, :, 2 * INNER :]

    padded = jnp.pad(enc_offsets, ((0, 0), (enc_total - enc_own, enc_total)))
    placed = lax.dynamic_slice_in_dim(padded, tensor_id * enc_own, 2 * enc_total - 1, 1)
    enc_table = jnp.dot(placed[:HEADS], onehot, precision=HIGH).T
    self_table = jnp.dot(
        lax.dot_general(
            self_gs.reshape(HEADS, -1).astype(F32), far_back, (((1,), (1,)), ((), ())),
            precision=HIGH,
        ),
        dec_onehot,
        precision=HIGH,
    ).T
    tables_local = jnp.stack([enc_table, self_table])
    gains_sum, tables_sum = lax.psum(((gains_b + gains_c)[:6], tables_local), ("dp", "tensor"))
    return (
        dec_out[:dec_own], enc_grad, dec_grad[:dec_own], gains_sum, tables_sum, qk_sum, vo_sum,
        ffin_sum, ffout_sum,
    )


def solution(mesh):
    rows = P(("dp", "tensor"), None)
    return jax.shard_map(
        on_device,
        mesh=mesh,
        in_specs=(
            rows, rows, rows, P("dp"), P("dp"), P("dp"), P(), P(), P(), P(), P(), P(),
            P(None, None, None, "tensor"), P(None, "tensor", None),
        ),
        out_specs=(
            rows, rows, rows, P(), P(), P(None, "dp", None), P(None, "dp", None),
            P(None, None, "dp", "tensor"), P(None, "tensor", "dp"),
        ),
        check_vma=False,
    )
```

time: 670 us -> 600 us (0.90)
  Pallas kernels: 0 us -> 137 us
  matrix products: 144 us -> 32 us
  local copies, waits for them, and re-layouts: 167 us -> 80.4 us
  waiting for transfers between devices: 130 us -> 206 us
  other arithmetic: 63.4 us -> 25.7 us
  blocking collectives: 78.2 us -> 41.3 us
    pallas_call x0 -> x3, Pallas kernels: none -> 137 us  [the longest x1 64.8 us: ka_call(): pl.pallas_call(ka_kernel, out_shape=outs, in_specs=[vmem] * 10 + [hbm] *...]
    dot_general x76 -> x24, matrix products: 144 us -> 32 us  [the longest x18 27.9 us: dot_first(): lax.dot_general(left, right, (((0,), (0,)), ((), ())), preferred_element_...]
    ppermute x18, waiting for transfers between devices: 40.2 us -> 113 us  [dp_sum(): other = lax.ppermute(send, 'dp', [(i, i ^ bit) for i in range(size)])]
    all_gather x5 -> x0, blocking collectives: 37.2 us -> none  [gather_t(): return lax.all_gather(rows, 'tensor', axis=0, tiled=True)]
    ppermute x9, waiting for transfers between devices: 49.6 us -> 82.9 us  [dp_sum(): other = lax.ppermute(send, 'dp', [(i, i ^ 1) for i in range(size)])]
    reshape x29 -> x1, local copies, waits for them, and re-layouts: 31.1 us -> 0.74 us  [prepare(): dec_mask.reshape(4, dec_own)]
    unnamed x366 -> x131, local copies, waits for them, and re-layouts: 29.3 us -> 8.1 us
    convert_element_type x32 -> x18, local copies, waits for them, and re-layouts: 24.1 us -> 7.56 us  [to_low(): return value.astype(LOW)]
  transfers between devices with their start and end apart: 43 -> 34, of which waited for: 16 -> 16; matrix products, arithmetic and copies ran while one was open for 39% -> 19% of each run, Pallas kernels for 0% -> 5%
where the time goes in v2:
time: 600 us; the launch traced here: 590 us
  waiting for transfers between devices  206 us (34%)
  Pallas kernels  137 us (23%)
  local copies, waits for them, and re-layouts  80.4 us (13%)
  starting transfers between devices  51.1 us (9%)
  blocking collectives  41.3 us (7%)
  matrix products  32 us (5%)
  other arithmetic  25.7 us (4%)
  between operations  16.2 us (3%)
    ppermute x18, waiting for transfers between devices, dp_sum(): other = lax.ppermute(send, 'dp', [(i, i ^ bit) for i in range(size)])  113 us
    ppermute x9, waiting for transfers between devices, dp_sum(): other = lax.ppermute(send, 'dp', [(i, i ^ 1) for i in range(size)])  82.9 us
    pallas_call x1, Pallas kernels, ka_call(): pl.pallas_call(ka_kernel, out_shape=outs, in_specs=[vmem] * 10 + [hbm] *...  64.8 us
    psum x1, blocking collectives, on_device(): lax.psum(((gains_b + gains_c)[:6], tables_local), ('dp', 'tensor'))  41.3 us
    pallas_call x1, Pallas kernels, kb_call(): pl.pallas_call(kb_kernel, out_shape=outs, in_specs=[vmem] * 13 + [hbm] *...  40.4 us
    pallas_call x1, Pallas kernels, kc_call(): pl.pallas_call(kc_kernel, out_shape=outs, in_specs=[vmem] * 14 + [hbm] *...  31.8 us
    dot_general x18, matrix products, dot_first(): lax.dot_general(left, right, (((0,), (0,)), ((), ())), preferred_element_...  27.9 us
    all_to_all x6, starting transfers between devices, to_owner(): out = lax.all_to_all(jnp.stack(pieces), 'tensor', 0, 0, tiled=True)  22 us
  transfers between devices with their start and end apart: 34, of which 16 were waited for; matrix products, arithmetic and copies ran while one was open for 19% of the time, Pallas kernels for 5%

profile of v2, /device:TPU:0, one launch (start us, length us, event | category | flops | bytes accessed | tf_op | source)
XLA Modules:
  0.0 589.8 jit_solution(211423408324023903)
XLA Ops:
  20.6 64.8 %forward_chain.1 = (bf16[128,1472]{1,0:T(8,128)(2,1)}, bf16[128,384]{1,0:T(8,128)(2,1)}, bf16[4,128,768]{2,1,0:T(8,128)(2,1)}, f32[6,128,512]{2,1,0:T(8,128)}, b...) custom-call(bf16[128,1472]{1,0:T(8,128)(2,1)} %copy.95.enc_x, ...), custom_call_target="tpu_custom_call" | custom-call | tf_op jit(solution)/shard_map/forward_chain/pallas_call | solution.py:412
  85.4 40.4 %middle_chain.1 = (bf16[32,1472]{1,0:T(8,128)(2,1)}, bf16[32,1472]{1,0:T(8,128)(2,1)}, bf16[32,384]{1,0:T(8,128)(2,1)}, bf16[128,768]{1,0:T(8,128)(2,1)}, f32[32...) custom-call(bf16[4,32,896]{2,1,0:T(8,128)(2,1)} %get-tuple-element.5, ...), custom_call_target="tpu_custom_call" | custom-call | tf_op jit(solution)/shard_map/middle_chain/pallas_call | solution.py:630
  150.3 31.8 %last_chain.1 = (f32[128,1472]{1,0:T(8,128)}, bf16[128,1472]{1,0:T(8,128)(2,1)}, bf16[128,384]{1,0:T(8,128)(2,1)}, bf16[128,768]{1,0:T(8,128)(2,1)}, f32[8,640]{...) custom-call(bf16[4,128,896]{2,1,0:T(8,128)(2,1)} %get-tuple-element., ...), custom_call_target="tpu_custom_call" | custom-call | tf_op jit(solution)/shard_map/last_chain/pallas_call | solution.py:773
  202.8 3.6 all-to-all-done.2
  206.4 4.3 all-to-all-start
  236.9 22.9 %collective-permute-done.3 = bf16[736,384]{1,0:T(8,128)(2,1)} collective-permute-done((bf16[736,384]{1,0:T(8,128)(2,1)}, bf16[736,384]{1,0:T(8,128)(2,1)}, u32[]{:S(2)}, u32[]{:S(2)}) %collective-permute-start.3) | collective-permute-done | bytes 565280 | tf_op jit(solution)/shard_map/ppermute | solution.py:812
  266.7 41.3 %all-reduce.9 = (f32[6,1472]{1,0:T(8,128)}, f32[2,32,6]{1,2,0:T(8,128)S(1)}) all-reduce(f32[6,1472]{1,0:T(8,128)} %slice_add_fusion, f32[2,32,6]{1,2,0:T(8,128)S(1)} %pad_maximum_fusion.9), channel_id=1, replica_groups=mesh['dp'=8,'tensor'=4] {'dp','tensor'}, use_global_device_ids=true, to_apply=%region_0.1 | all-reduce | flops 9216 | bytes 73728 | tf_op jit(solution)/shard_map/psum | solution.py:910
  313.8 3.7 all-to-all-start.1
  319.6 7.4 %copy.100 = bf16[4,128,1472]{1,0,2:T(4,128)(2,1)} copy(bf16[4,128,1472]{1,2,0:T(8,128)(2,1)} %all-to-all-done) | data formatting | bytes 3014656 | tf_op jit(solution)/shard_map/all_to_all | solution.py:827
  327.0 3.7 reshape_reshape.59
  335.6 7.9 %copy.106 = bf16[4,128,1472]{1,0,2:T(4,128)(2,1)} copy(bf16[4,128,1472]{1,2,0:T(8,128)(2,1)S(1)} %all-to-all-done.4) | data formatting | bytes 3014656 | tf_op jit(solution)/shard_map/all_to_all | solution.py:827
  352.7 4.5 all-to-all-done.5
  374.0 16.0 %collective-permute-done.15 = bf16[736,896]{1,0:T(8,128)(2,1)S(1)} collective-permute-done((bf16[736,896]{1,0:T(8,128)(2,1)}, bf16[736,896]{1,0:T(8,128)(2,1)S(1)}, u32[]{:S(2)}, u32[]{:S(2)}) %collective-permute-start.15) | collective-permute-done | bytes 1318944 | tf_op jit(solution)/shard_map/ppermute | solution.py:812
  392.1 26.2 %collective-permute-done.18 = bf16[736,896]{1,0:T(8,128)(2,1)S(1)} collective-permute-done((bf16[736,896]{1,0:T(8,128)(2,1)}, bf16[736,896]{1,0:T(8,128)(2,1)S(1)}, u32[]{:S(2)}, u32[]{:S(2)}) %collective-permute-start.18) | collective-permute-done | bytes 1318944 | tf_op jit(solution)/shard_map/ppermute | solution.py:812
  421.4 9.0 %collective-permute-done = bf16[736,384]{1,0:T(8,128)(2,1)S(1)} collective-permute-done((bf16[736,384]{1,0:T(8,128)(2,1)S(1)}, bf16[736,384]{1,0:T(8,128)(2,1)S(1)}, u32[]{:S(2)}, u32[]{:S(2)}) %collective-permute-start) | collective-permute-done | bytes 565280 | tf_op jit(solution)/shard_map/ppermute | solution.py:812
  432.6 8.8 %collective-permute-done.6 = bf16[736,384]{1,0:T(8,128)(2,1)S(1)} collective-permute-done((bf16[736,384]{1,0:T(8,128)(2,1)S(1)}, bf16[736,384]{1,0:T(8,128)(2,1)S(1)}, u32[]{:S(2)}, u32[]{:S(2)}) %collective-permute-start.6) | collective-permute-done | bytes 565280 | tf_op jit(solution)/shard_map/ppermute | solution.py:812
  451.9 18.4 %collective-permute-done.16 = bf16[2,184,896]{2,1,0:T(8,128)(2,1)S(1)} collective-permute-done((bf16[2,184,896]{2,1,0:T(8,128)(2,1)S(1)}, bf16[2,184,896]{2,1,0:T(8,128)(2,1)S(1)}, u32[]{:S(2)}, u32[]{:S(2)}) %collective-permute-start.16) | collective-permute-done | bytes 659488 | tf_op jit(solution)/shard_map/ppermute | solution.py:820
  471.5 26.0 %collective-permute-done.1 = bf16[2,184,384]{2,1,0:T(8,128)(2,1)S(1)} collective-permute-done((bf16[2,184,384]{2,1,0:T(8,128)(2,1)S(1)}, bf16[2,184,384]{2,1,0:T(8,128)(2,1)S(1)}, u32[]{:S(2)}, u32[]{:S(2)}) %collective-permute-start.1) | collective-permute-done | bytes 282656 | tf_op jit(solution)/shard_map/ppermute | solution.py:820
  497.6 4.1 collective-permute-done.7
  501.8 21.1 %collective-permute-done.2 = bf16[1,184,384]{2,1,0:T(8,128)(2,1)S(1)} collective-permute-done((bf16[1,184,384]{2,1,0:T(8,128)(2,1)S(1)}, bf16[1,184,384]{2,1,0:T(8,128)(2,1)S(1)}, u32[]{:S(2)}, u32[]{:S(2)}) %collective-permute-start.2) | collective-permute-done | bytes 141344 | tf_op jit(solution)/shard_map/ppermute | solution.py:820
  523.0 9.2 %collective-permute-done.8 = bf16[1,184,384]{2,1,0:T(8,128)(2,1)S(1)} collective-permute-done((bf16[1,184,384]{2,1,0:T(8,128)(2,1)S(1)}, bf16[1,184,384]{2,1,0:T(8,128)(2,1)S(1)}, u32[]{:S(2)}, u32[]{:S(2)}) %collective-permute-start.8) | collective-permute-done | bytes 141344 | tf_op jit(solution)/shard_map/ppermute | solution.py:820
  540.9 22.3 %collective-permute-done.14 = bf16[1,184,896]{2,1,0:T(8,128)(2,1)} collective-permute-done((bf16[1,184,896]{2,1,0:T(8,128)(2,1)}, bf16[1,184,896]{2,1,0:T(8,128)(2,1)}, u32[]{:S(2)}, u32[]{:S(2)}) %collective-permute-start.14) | collective-permute-done | bytes 329760 | tf_op jit(solution)/shard_map/ppermute | solution.py:820
  565.5 4.7 collective-permute-done.17
  570.3 6.9 %collective-permute-done.20 = bf16[1,184,896]{2,1,0:T(8,128)(2,1)S(1)} collective-permute-done((bf16[1,184,896]{2,1,0:T(8,128)(2,1)S(1)}, bf16[1,184,896]{2,1,0:T(8,128)(2,1)S(1)}, u32[]{:S(2)}, u32[]{:S(2)}) %collective-permute-start.20) | collective-permute-done | bytes 329760 | tf_op jit(solution)/shard_map/ppermute | solution.py:820
  (305 shorter events, 164.4 us)
Async XLA Ops:
  133.0 227.0 %collective-permute-start.21 = (bf16[736,896]{1,0:T(8,128)(2,1)}, bf16[736,896]{1,0:T(8,128)(2,1)}, u32[]{:S(2)}, u32[]{:S(2)}) collective-permute-start(bf16[736,896]{1,0:T(8,128)(2,1)} %convolution_convert_fusion.1), channel_id=1, source_target_pairs={{0,4},{4,0},{8,12},{12,8},{16,20},{20,16},{24,28},{28,24},{1,5},{5... | collective-permute-start | bytes 3956744 | tf_op jit(solution)/shard_map/ppermute | solution.py:812
  138.5 224.4 %collective-permute-start.24 = (bf16[736,896]{1,0:T(8,128)(2,1)}, bf16[736,896]{1,0:T(8,128)(2,1)}, u32[]{:S(2)}, u32[]{:S(2)}) collective-permute-start(bf16[736,896]{1,0:T(8,128)(2,1)} %convolution_convert_fusion), channel_id=1, source_target_pairs={{0,4},{4,0},{8,12},{12,8},{16,20},{20,16},{24,28},{28,24},{1,5},{5... | collective-permute-start | bytes 3956744 | tf_op jit(solution)/shard_map/ppermute | solution.py:812
  146.3 220.3 %collective-permute-start.9 = (bf16[736,896]{1,0:T(8,128)(2,1)}, bf16[736,896]{1,0:T(8,128)(2,1)}, u32[]{:S(2)}, u32[]{:S(2)}) collective-permute-start(bf16[736,896]{1,0:T(8,128)(2,1)} %convolution_convert_fusion.5), channel_id=1, source_target_pairs={{0,4},{4,0},{8,12},{12,8},{16,20},{20,16},{24,28},{28,24},{1,5},{5... | collective-permute-start | bytes 3956744 | tf_op jit(solution)/shard_map/ppermute | solution.py:812
  149.8 220.2 %collective-permute-start.12 = (bf16[736,896]{1,0:T(8,128)(2,1)}, bf16[736,896]{1,0:T(8,128)(2,1)}, u32[]{:S(2)}, u32[]{:S(2)}) collective-permute-start(bf16[736,896]{1,0:T(8,128)(2,1)} %convolution_convert_fusion.4), channel_id=1, source_target_pairs={{0,4},{4,0},{8,12},{12,8},{16,20},{20,16},{24,28},{28,24},{1,5},{5... | collective-permute-start | bytes 3956744 | tf_op jit(solution)/shard_map/ppermute | solution.py:812
  221.9 37.9 %collective-permute-start.3 = (bf16[736,384]{1,0:T(8,128)(2,1)}, bf16[736,384]{1,0:T(8,128)(2,1)}, u32[]{:S(2)}, u32[]{:S(2)}) collective-permute-start(bf16[736,384]{1,0:T(8,128)(2,1)} %convolution_convert_fusion.8), channel_id=1, source_target_pairs={{0,4},{4,0},{8,12},{12,8},{16,20},{20,16},{24,28},{28,24},{1,5},{5... | collective-permute-start | bytes 1695752 | tf_op jit(solution)/shard_map/ppermute | solution.py:812
  230.2 83.6 %all-to-all-start.4 = ((bf16[4,128,1472]{1,2,0:T(8,128)(2,1)}), bf16[4,128,1472]{1,2,0:T(8,128)(2,1)S(1)}, u32[]{:S(2)}, u32[]{:S(2)}) async-start(bf16[4,128,1472]{1,2,0:T(8,128)(2,1)} %copy.105), calls=%async_computation.4 | async-start | bytes 3014656 | tf_op jit(solution)/shard_map/all_to_all | solution.py:827
  263.0 54.5 %collective-permute-start.4 = (bf16[2,184,384]{2,1,0:T(8,128)(2,1)}, bf16[2,184,384]{2,1,0:T(8,128)(2,1)}, u32[]{:S(2)}, u32[]{:S(2)}) collective-permute-start(bf16[2,184,384]{2,1,0:T(8,128)(2,1)} %fusion.12), channel_id=1, source_target_pairs={{0,8},{4,12},{8,0},{12,4},{16,24},{20,28},{24,16},{28,20},{1,9},{5... | collective-permute-start | bytes 847880 | tf_op jit(solution)/shard_map/ppermute | solution.py:820
  313.8 32.4 %all-to-all-start.1 = ((bf16[4,128,384]{2,1,0:T(8,128)(2,1)}), bf16[4,128,384]{2,1,0:T(8,128)(2,1)S(1)}, u32[]{:S(2)}, u32[]{:S(2)}) async-start(bf16[4,128,384]{2,1,0:T(8,128)(2,1)} %pad_maximum_fusion.5), calls=%async_computation.1 | async-start | bytes 786432 | tf_op jit(solution)/shard_map/all_to_all | solution.py:827
  349.8 229.3 %all-gather.2.cloned.1.call-start = ((), (), s32[]{:S(2)}) async-start(), calls=%async_computation.6 | async-start | bytes 2119680 | tf_op jit(solution)/shard_map/all_gather | solution.py:892
  357.8 32.2 %collective-permute-start.15 = (bf16[736,896]{1,0:T(8,128)(2,1)}, bf16[736,896]{1,0:T(8,128)(2,1)S(1)}, u32[]{:S(2)}, u32[]{:S(2)}) collective-permute-start(bf16[736,896]{1,0:T(8,128)(2,1)} %convolution_convert_fusion.3), channel_id=1, source_target_pairs={{0,4},{4,0},{8,12},{12,8},{16,20},{20,16},{24,28},{28,24},{1,5},{5... | collective-permute-start | bytes 3956744 | tf_op jit(solution)/shard_map/ppermute | solution.py:812
  360.0 58.2 %collective-permute-start.18 = (bf16[736,896]{1,0:T(8,128)(2,1)}, bf16[736,896]{1,0:T(8,128)(2,1)S(1)}, u32[]{:S(2)}, u32[]{:S(2)}) collective-permute-start(bf16[736,896]{1,0:T(8,128)(2,1)} %convolution_convert_fusion.2), channel_id=1, source_target_pairs={{0,4},{4,0},{8,12},{12,8},{16,20},{20,16},{24,28},{28,24},{1,5},{5... | collective-permute-start | bytes 3956744 | tf_op jit(solution)/shard_map/ppermute | solution.py:812
  362.9 67.5 %collective-permute-start = (bf16[736,384]{1,0:T(8,128)(2,1)S(1)}, bf16[736,384]{1,0:T(8,128)(2,1)S(1)}, u32[]{:S(2)}, u32[]{:S(2)}) collective-permute-start(bf16[736,384]{1,0:T(8,128)(2,1)S(1)} %copy-done.36), channel_id=1, source_target_pairs={{0,4},{4,0},{8,12},{12,8},{16,20},{20,16},{24,28},{28,24},{1,5},{5... | collective-permute-start | bytes 1695752 | tf_op jit(solution)/shard_map/ppermute | solution.py:812
  366.6 74.8 %collective-permute-start.6 = (bf16[736,384]{1,0:T(8,128)(2,1)S(1)}, bf16[736,384]{1,0:T(8,128)(2,1)S(1)}, u32[]{:S(2)}, u32[]{:S(2)}) collective-permute-start(bf16[736,384]{1,0:T(8,128)(2,1)S(1)} %convolution_convert_fusion.6), channel_id=1, source_target_pairs={{0,4},{4,0},{8,12},{12,8},{16,20},{20,16},{24,28},{28,24},{1,5},{5... | collective-permute-start | bytes 1695752 | tf_op jit(solution)/shard_map/ppermute | solution.py:812
  370.0 73.7 %collective-permute-start.22 = (bf16[2,184,896]{2,1,0:T(8,128)(2,1)S(1)}, bf16[2,184,896]{2,1,0:T(8,128)(2,1)S(1)}, u32[]{:S(2)}, u32[]{:S(2)}) collective-permute-start(bf16[2,184,896]{2,1,0:T(8,128)(2,1)S(1)} %fusion.9), channel_id=1, source_target_pairs={{0,8},{4,12},{8,0},{12,4},{16,24},{20,28},{24,16},{28,20},{1,9},{5... | collective-permute-start | bytes 1978376 | tf_op jit(solution)/shard_map/ppermute | solution.py:820
  390.0 54.3 %collective-permute-start.25 = (bf16[2,184,896]{2,1,0:T(8,128)(2,1)S(1)}, bf16[2,184,896]{2,1,0:T(8,128)(2,1)S(1)}, u32[]{:S(2)}, u32[]{:S(2)}) collective-permute-start(bf16[2,184,896]{2,1,0:T(8,128)(2,1)S(1)} %fusion.10), channel_id=1, source_target_pairs={{0,8},{4,12},{8,0},{12,4},{16,24},{20,28},{24,16},{28,20},{1,9},{5... | collective-permute-start | bytes 1978376 | tf_op jit(solution)/shard_map/ppermute | solution.py:820
  443.7 90.5 %collective-permute-start.19 = (bf16[2,184,896]{2,1,0:T(8,128)(2,1)}, bf16[2,184,896]{2,1,0:T(8,128)(2,1)S(1)}, u32[]{:S(2)}, u32[]{:S(2)}) collective-permute-start(bf16[2,184,896]{2,1,0:T(8,128)(2,1)} %fusion.8), channel_id=1, source_target_pairs={{0,8},{4,12},{8,0},{12,4},{16,24},{20,28},{24,16},{28,20},{1,9},{5... | collective-permute-start | bytes 1978376 | tf_op jit(solution)/shard_map/ppermute | solution.py:820
  444.3 53.2 %collective-permute-start.1 = (bf16[2,184,384]{2,1,0:T(8,128)(2,1)S(1)}, bf16[2,184,384]{2,1,0:T(8,128)(2,1)S(1)}, u32[]{:S(2)}, u32[]{:S(2)}) collective-permute-start(bf16[2,184,384]{2,1,0:T(8,128)(2,1)S(1)} %fusion.11), channel_id=1, source_target_pairs={{0,8},{4,12},{8,0},{12,4},{16,24},{20,28},{24,16},{28,20},{1,9},{5... | collective-permute-start | bytes 847880 | tf_op jit(solution)/shard_map/ppermute | solution.py:820
  446.1 55.6 %collective-permute-start.7 = (bf16[2,184,384]{2,1,0:T(8,128)(2,1)S(1)}, bf16[2,184,384]{2,1,0:T(8,128)(2,1)S(1)}, u32[]{:S(2)}, u32[]{:S(2)}) collective-permute-start(bf16[2,184,384]{2,1,0:T(8,128)(2,1)S(1)} %fusion.13), channel_id=1, source_target_pairs={{0,8},{4,12},{8,0},{12,4},{16,24},{20,28},{24,16},{28,20},{1,9},{5... | collective-permute-start | bytes 847880 | tf_op jit(solution)/shard_map/ppermute | solution.py:820
  449.2 88.2 %collective-permute-start.23 = (bf16[1,184,896]{2,1,0:T(8,128)(2,1)}, bf16[1,184,896]{2,1,0:T(8,128)(2,1)}, u32[]{:S(2)}, u32[]{:S(2)}) collective-permute-start(bf16[1,184,896]{2,1,0:T(8,128)(2,1)} %dynamic-slice_convert_fusion.1), channel_id=1, source_target_pairs={{0,16},{4,20},{8,24},{12,28},{16,0},{20,4},{24,8},{28,12},{1,17},{... | collective-permute-start | bytes 989192 | tf_op jit(solution)/shard_map/ppermute | solution.py:820
  470.3 68.4 %collective-permute-start.26 = (bf16[1,184,896]{2,1,0:T(8,128)(2,1)}, bf16[1,184,896]{2,1,0:T(8,128)(2,1)}, u32[]{:S(2)}, u32[]{:S(2)}) collective-permute-start(bf16[1,184,896]{2,1,0:T(8,128)(2,1)} %dynamic-slice_convert_fusion), channel_id=1, source_target_pairs={{0,16},{4,20},{8,24},{12,28},{16,0},{20,4},{24,8},{28,12},{1,17},{... | collective-permute-start | bytes 989192 | tf_op jit(solution)/shard_map/ppermute | solution.py:820
  497.5 42.3 %collective-permute-start.11 = (bf16[1,184,896]{2,1,0:T(8,128)(2,1)}, bf16[1,184,896]{2,1,0:T(8,128)(2,1)}, u32[]{:S(2)}, u32[]{:S(2)}) collective-permute-start(bf16[1,184,896]{2,1,0:T(8,128)(2,1)} %dynamic-slice_convert_fusion.5), channel_id=1, source_target_pairs={{0,16},{4,20},{8,24},{12,28},{16,0},{20,4},{24,8},{28,12},{1,17},{... | collective-permute-start | bytes 989192 | tf_op jit(solution)/shard_map/ppermute | solution.py:820
  532.1 31.1 %collective-permute-start.14 = (bf16[1,184,896]{2,1,0:T(8,128)(2,1)}, bf16[1,184,896]{2,1,0:T(8,128)(2,1)}, u32[]{:S(2)}, u32[]{:S(2)}) collective-permute-start(bf16[1,184,896]{2,1,0:T(8,128)(2,1)} %dynamic-slice_convert_fusion.4), channel_id=1, source_target_pairs={{0,16},{4,20},{8,24},{12,28},{16,0},{20,4},{24,8},{28,12},{1,17},{... | collective-permute-start | bytes 989192 | tf_op jit(solution)/shard_map/ppermute | solution.py:820
  534.2 36.0 %collective-permute-start.17 = (bf16[1,184,896]{2,1,0:T(8,128)(2,1)S(1)}, bf16[1,184,896]{2,1,0:T(8,128)(2,1)S(1)}, u32[]{:S(2)}, u32[]{:S(2)}) collective-permute-start(bf16[1,184,896]{2,1,0:T(8,128)(2,1)S(1)} %dynamic-slice_convert_fusion.3), channel_id=1, source_target_pairs={{0,16},{4,20},{8,24},{12,28},{16,0},{20,4},{24,8},{28,12},{1,17},{... | collective-permute-start | bytes 989192 | tf_op jit(solution)/shard_map/ppermute | solution.py:820
  537.4 39.8 %collective-permute-start.20 = (bf16[1,184,896]{2,1,0:T(8,128)(2,1)S(1)}, bf16[1,184,896]{2,1,0:T(8,128)(2,1)S(1)}, u32[]{:S(2)}, u32[]{:S(2)}) collective-permute-start(bf16[1,184,896]{2,1,0:T(8,128)(2,1)S(1)} %dynamic-slice_convert_fusion.2), channel_id=1, source_target_pairs={{0,16},{4,20},{8,24},{12,28},{16,0},{20,4},{24,8},{28,12},{1,17},{... | collective-permute-start | bytes 989192 | tf_op jit(solution)/shard_map/ppermute | solution.py:820
  (74 other events, 828.5 us)
Sparse Core Ops, SparseCore 0:
  533.2 20.2 all-gather.1
